TPU v7x, 32 devices: a whole 2x2x4 slice. The times are simulated.
32 devices in a mesh: blk: 4 (over y, x), grp: 8 (over z, core).
Axes of the slice: x: 2, y: 2, z: 4, core: 2. Of those that a mesh axis runs over, the one named last changes fastest.
Arguments:
- record: bfloat16 [16448, 8192], P(None, ('blk', 'grp')), may hold values from -400 to 400
- owner_order: int32 [4, 4], replicated, may hold values from 0 to 7, as said below
Outputs:
- cross_spectra: bfloat16 [4, 2, 16, 8192, 256], P(None, None, None, ('blk', 'grp'))
Inputs may be any that keep to these rules, and one draw needn't show every extreme that they name: `owner_order`: a channel block position within a group.
All inputs are finite; a program needn't handle non-finite values.
Results may differ from a plain program's by a relative error of at most 0.0071.
Values may be sent and summed in bfloat16 or wider, within the bound.
No kernel may reach another device: no remote copies, remote signals or barrier semaphores. Data moves between devices by JAX's collectives and lax.ppermute only.
A program may use at most 192 MiB of HBM per device.

v0:
```python
import functools
import math

import jax
import jax.numpy as jnp
import numpy as np
from jax import lax
from jax.experimental import pallas as pl
from jax.experimental.pallas import tpu as pltpu
from jax.sharding import PartitionSpec as P

WIN = 256
NS = 128
NB = 16
BIN_LO = 8
ROUNDS = 4
HOP = 64
WG = 16
CORES = 2
HALF = NB // CORES
FIRST = 4
GROUP = 4
PICK = 3
GIVE = 5
TAIL = (2, 5, 9, 11)
PARTS, TURN = 2, (5, 7)
GAP = 5
REST_AT = 1
LAG = 2
ORDER = ((1, 0), (1, 1), (3, 0), (3, 1), (2, 0), (2, 1), (0, 0), (0, 1))
VMEM = 8 * 2**20
SHORT = pl.CostEstimate(flops=1, bytes_accessed=1, transcendentals=0)


def band_table():
    n = np.arange(NS)
    q = BIN_LO + np.arange(NB)
    phase = ((q[:, None] * n[None, :]) % NS) * (2.0 * math.pi / NS)
    taper = 0.5 - 0.5 * np.cos(n * (2.0 * math.pi / NS))
    scale = 1.0 / math.sqrt(3.0 * NS / 8.0)
    real = taper * np.cos(phase) * scale
    imag = -taper * np.sin(phase) * scale
    return np.stack([real, imag], axis=1).astype(np.float32)


def tables(lo, hi):
    table = band_table().reshape(CORES, HALF, 2, NS)[:, lo:hi].swapaxes(0, 1)
    out = np.stack([np.roll(table, w * HOP, axis=-1) for w in range(WG)], axis=-2)
    return jnp.asarray(out.reshape(-1, NS).astype(jnp.bfloat16))


def in_hbm():
    return pl.BlockSpec(memory_space=pltpu.MemorySpace.HBM)


def token_shape():
    return jax.ShapeDtypeStruct((8, 128), jnp.int32)


def in_place():
    return pl.BlockSpec(memory_space=pl.ANY)


def half_energy(x):
    wide = x.astype(jnp.float32)
    return jnp.sum((wide * wide).reshape(-1, HOP, x.shape[-1]), axis=1)


def band_kernel(first, core_ref, main_ref, halo_ref, rows_ref, *refs):
    *refs, table = refs

    @pl.when(pl.program_id(0) == 0)
    def _():
        rows = rows_ref[...].astype(jnp.float32)
        start = (lax.broadcasted_iota(jnp.int32, rows.shape, 0) & (WG - 1)) * HOP
        lane = lax.broadcasted_iota(jnp.int32, rows.shape, 1)
        for at in range(0, table.shape[1], NS):
            sample = lane + at - start
            table[:, at : at + NS] = jnp.where((sample >= 0) & (sample < NS), rows, 0.0).astype(jnp.bfloat16)

    main, halo = main_ref[...], halo_ref[...]
    if first:
        out, inv_ref, _ = refs
        energy = half_energy(main)
        later = jnp.concatenate([energy[1:], half_energy(halo)], axis=0)
        inv = 1.0 / jnp.sqrt((energy + later) / NS + 1e-05)
        inv_ref[...] = inv
    else:
        inv_ref, _, out, _ = refs
        inv = inv_ref[...]
    split = WG * HOP
    raw = jnp.dot(table[:, :split], main, preferred_element_type=jnp.float32)
    raw += jnp.dot(table[:, split : split + HOP], halo, preferred_element_type=jnp.float32)
    raw = raw.reshape(-1, CORES, 2, WG, main.shape[1])
    out[...] = (raw * inv).astype(jnp.bfloat16)


def band(core, record, lo, hi, inv=None, token=None):
    channels = record.shape[1]
    table = tables(lo, hi)
    rows, width = table.shape[0], (WG // 2 + 1) * NS
    first = inv is None
    inv_spec = pl.BlockSpec((WG, channels), lambda i: (i, 0))
    in_specs = [
        pl.BlockSpec(memory_space=pltpu.SMEM),
        pl.BlockSpec((WG * HOP, channels), lambda i: (i, 0)),
        pl.BlockSpec((HOP, channels), lambda i: ((i + 1) * WG, 0)),
        pl.BlockSpec(table.shape, lambda i: (0, 0)),
    ]
    out_specs = [pl.BlockSpec((hi - lo, CORES, 2, WG, channels), lambda i: (0, 0, 0, i, 0))]
    out_shape = [jax.ShapeDtypeStruct((hi - lo, CORES, 2, WIN, channels), jnp.bfloat16)]
    args = [core, record, record, table]
    if first:
        out_specs.append(inv_spec)
        out_shape.append(jax.ShapeDtypeStruct((WIN, channels), jnp.float32))
    else:
        in_specs += [inv_spec, in_place()]
        args += [inv, token]
    return pl.pallas_call(
        functools.partial(band_kernel, first),
        grid=(WIN // WG,),
        in_specs=in_specs,
        out_specs=out_specs + [in_place()],
        out_shape=out_shape + [token_shape()],
        scratch_shapes=[pltpu.VMEM((rows, width), jnp.bfloat16)],
        name="band_first" if first else "band_rest",
        compiler_params=pltpu.CompilerParams(vmem_limit_bytes=VMEM),
        cost_estimate=pl.CostEstimate(
            flops=2 * rows * (WIN // WG) * width * channels, bytes_accessed=3 * record.size, transcendentals=0
        ),
    )(*args)


def turn_kernel(in_ref, _, out_ref, __):
    for part in range(2):
        out_ref[0, 0, :, part * WIN : (part + 1) * WIN] = in_ref[0, 0, part].T


def turn(spectra, token):
    count, channels = spectra.shape[0], spectra.shape[-1]
    return pl.pallas_call(
        turn_kernel,
        grid=(count, CORES),
        in_specs=[pl.BlockSpec((1, 1, 2, WIN, channels), lambda i, h: (i, h, 0, 0, 0)), in_place()],
        out_specs=[pl.BlockSpec((1, 1, channels, 2 * WIN), lambda i, h: (i, h, 0, 0)), in_place()],
        out_shape=[jax.ShapeDtypeStruct((count, CORES, channels, 2 * WIN), jnp.bfloat16), token_shape()],
        name="turn",
        compiler_params=pltpu.CompilerParams(vmem_limit_bytes=VMEM),
        cost_estimate=SHORT,
    )(spectra, token)


def place(arrays, a):
    for i, b in enumerate(arrays):
        if b is a:
            return i
    arrays.append(a)
    return len(arrays) - 1


def seat():
    member = lax.axis_index("grp")
    return lax.axis_index("blk"), member // CORES, member % CORES, lax.axis_size("grp") // CORES


def chunk_of(k):
    r, half = ORDER[k // GROUP]
    return r, half * GROUP + k % GROUP


def asked_of(orders, k):
    r, _ = chunk_of(k)
    return orders[r, lax.rem(lax.axis_index("blk") + r, lax.axis_size("blk"))]


def inject(orders, token, step, mine, twin, held):
    chips = lax.axis_size("grp") // CORES
    sent = [step - LAG * hop for hop in range(chips)]
    hops = [hop for hop in range(chips) if 0 <= sent[hop] < ROUNDS * HALF]
    arrays, slots = [], {}
    for hop in hops:
        _, row = chunk_of(sent[hop])
        slots[hop] = (place(arrays, mine[row // FIRST]), row % FIRST), (place(arrays, twin[row]), None)
    whole = twin[0].shape

    def kernel(orders_ref, *refs):
        ins, out, buffer, sem = refs[: len(arrays)], refs[-4], refs[-2], refs[-1]
        _, chip, core, _ = seat()
        seen = jnp.where(core == 0, chip, chips - 1 - chip)
        for hop in hops:
            owner = asked_of(orders_ref, sent[hop])
            here = (seen == hop) & (owner // CORES == chip)
            for (slot, row), same in zip(slots[hop], (True, False), strict=True):
                source = ins[slot] if row is None else ins[slot].at[row]

                @pl.when(here & ((owner % CORES == core) == same))
                def _(source=source):
                    load = pltpu.make_async_copy(source, buffer, sem.at[0])
                    load.start()
                    load.wait()
                    store = pltpu.make_async_copy(buffer, out, sem.at[1])
                    store.start()
                    store.wait()

    in_specs = [pl.BlockSpec(memory_space=pltpu.SMEM)] + [in_hbm()] * len(arrays) + [in_place()]
    args = [orders, *arrays, token]
    aliases = {}
    if held is not None:
        in_specs.append(in_place())
        args.append(held)
        aliases = {len(args) - 1: 0}
    return pl.pallas_call(
        kernel,
        in_specs=in_specs,
        out_specs=[in_place()] * 2,
        out_shape=[jax.ShapeDtypeStruct(whole, jnp.bfloat16), token_shape()],
        input_output_aliases=aliases,
        scratch_shapes=[pltpu.VMEM(whole, jnp.bfloat16), pltpu.SemaphoreType.DMA((2,))],
        name="inject",
        compiler_params=pltpu.CompilerParams(vmem_limit_bytes=4 * 2**20),
        cost_estimate=SHORT,
    )(*args)


def gather(orders, token, ks, held, swapped=None):
    arrays = []
    chips = lax.axis_size("grp") // CORES
    slots = {(k, j): place(arrays, held[k + LAG * j]) for k in ks for j in range(chips - 1)}
    extra = [] if swapped is None else swapped
    apart = swapped is None
    shape = held[0].shape[1:]

    def kernel(orders_ref, *refs):
        ins, sems = refs[: len(arrays)], refs[-1]
        outs = refs[-2 - len(ks) : -2] if apart else [refs[-3].at[m] for m in range(len(ks))]
        _, chip, core, _ = seat()
        hop = jnp.where(core == 0, chip, chips - 1 - chip)
        home = asked_of(orders_ref, ks[0]) // CORES
        has = (hop >= 1) & ((home == chip) | ((core == 0) == (home < chip)))
        half = 1 - core if apart else core
        lead = jnp.maximum(hop, 1) - 1
        for j in range(chips - 1):

            @pl.when((lead == j) & (lead == j if apart else has))
            def _(j=j):
                for m, k in enumerate(ks):
                    pltpu.make_async_copy(ins[slots[k, j]].at[half], outs[m], sems.at[m]).start()

        if not apart:

            @pl.when(jnp.logical_not(has))
            def _():
                for m in range(len(ks)):
                    pltpu.make_async_copy(refs[len(arrays) + m], outs[m], sems.at[m]).start()

        for m in range(len(ks)):
            pltpu.make_async_copy(outs[m], outs[m], sems.at[m]).wait()

    in_vmem = pl.BlockSpec(memory_space=pltpu.VMEM)
    if apart:
        out_specs, out_shape = [in_vmem] * len(ks), [jax.ShapeDtypeStruct(shape, jnp.bfloat16)] * len(ks)
    else:
        out_specs, out_shape = [in_vmem], [jax.ShapeDtypeStruct((len(ks), *shape), jnp.bfloat16)]
    return pl.pallas_call(
        kernel,
        in_specs=[pl.BlockSpec(memory_space=pltpu.SMEM)] + [in_place()] * (len(arrays) + len(extra) + 1),
        out_specs=out_specs + [in_place()],
        out_shape=out_shape + [token_shape()],
        scratch_shapes=[pltpu.SemaphoreType.DMA((len(ks),))],
        name="collect" if apart else "select",
        compiler_params=pltpu.CompilerParams(vmem_limit_bytes=8 * 2**20),
        cost_estimate=SHORT,
    )(orders, *arrays, *extra, token)


def cross_kernel(core_ref, own_ref, near_ref, far_ref, *refs):
    out_ref = refs[-2]

    def emit(paired_ref):
        own = own_ref[0, 0]
        turned = jnp.concatenate([own[:, WIN:], -own[:, :WIN]], axis=1)
        paired = paired_ref[0].reshape(2 * WIN, -1)
        scale = 1.0 / math.sqrt(WIN)
        for part, lhs in enumerate((own, turned)):
            total = jnp.dot(lhs, paired, preferred_element_type=jnp.float32)
            out_ref[0, part, 0] = (total * scale).astype(jnp.bfloat16)

    @pl.when(pl.program_id(1) == 0)
    def _():
        emit(near_ref)

    @pl.when(pl.program_id(1) == 1)
    def _():
        emit(far_ref)


def cross(out, token, core, own, near, far, round_index, first_chunk, begin, count):
    channels = near.shape[-1]
    first_chunk += begin
    row = first_chunk % own.shape[0]
    paired_spec = pl.BlockSpec((1, 2, WIN, channels), lambda i, g, c: (begin + i, 0, 0, 0))
    in_specs = [
        pl.BlockSpec((1, 1, channels, 2 * WIN), lambda i, g, c: (row + i, (c[0] + g) % CORES, 0, 0)),
        paired_spec,
        paired_spec,
        in_place(),
    ]
    out_spec = pl.BlockSpec(
        (1, 2, 1, channels, channels),
        lambda i, g, c: (round_index, 0, ((c[0] + g) % CORES) * HALF + first_chunk + i, 0, 0),
    )
    args = [core, own, near, far, token]
    aliases = {}
    if out is not None:
        in_specs.append(in_place())
        args.append(out)
        aliases = {len(args) - 1: 0}
    return pl.pallas_call(
        cross_kernel,
        grid_spec=pltpu.PrefetchScalarGridSpec(
            num_scalar_prefetch=1, grid=(count, CORES), in_specs=in_specs, out_specs=[out_spec, in_place()]
        ),
        out_shape=[jax.ShapeDtypeStruct((ROUNDS, 2, NB, channels, channels), jnp.bfloat16), token_shape()],
        input_output_aliases=aliases,
        name="cross",
        compiler_params=pltpu.CompilerParams(vmem_limit_bytes=VMEM),
        cost_estimate=SHORT,
    )(*args)


def body(record, owner_order):
    groups, members = lax.axis_size("blk"), lax.axis_size("grp")
    chips = members // CORES
    core_arg = (lax.axis_index("grp") % CORES).reshape(1).astype(jnp.int32)

    flow = [(m, m + CORES) for m in range(0, members - CORES, CORES)]
    flow += [(m + CORES, m) for m in range(1, members - CORES, CORES)]
    swap = [(m, m ^ 1) for m in range(members)]
    chunks = ROUNDS * HALF
    steps = chunks + LAG * (chips - 2)

    mine_a, inv, token = band(core_arg, record, 0, FIRST)
    mine, twin = [mine_a], [lax.ppermute(mine_a[i], "grp", swap) for i in range(FIRST)]

    arrived, held, turned = [], [], []
    out = None
    kept, nears, fars = {}, {}, {}
    todo = {}
    for g in range(chunks // GROUP):
        at = (g + 1) * GROUP - 1 + LAG * (chips - 2) + LAG
        across = bool(ORDER[g][0])
        left = chunks // GROUP - 1 - g
        pick = at + (1 if left == 0 else PICK)
        give = pick + GIVE if across else pick
        meet = at + TAIL[left] if left < 4 else give + GAP
        plan = ((at, "collect", 0), (pick, "select", 0), (give, "pass_over", 0), *((meet + i * (left >= 4), "cross", i) for i in range(PARTS)))
        for wait, what, part in plan:
            todo.setdefault(wait, []).append((what, g, part))

    for step in range(max(todo) + 1):
        if step < steps + LAG:
            buffer = arrived[step - LAG] if step >= LAG else None
            sent, token = inject(owner_order, token, step, mine, twin, buffer)
            if step < steps:
                arrived.append(lax.ppermute(sent, "grp", flow))
            if step >= LAG:
                held.append(sent)
        if step == REST_AT:
            mine_b, token = band(core_arg, record, FIRST, HALF, inv, token)
            mine.append(mine_b)
            twin += [lax.ppermute(mine_b[i], "grp", swap) for i in range(HALF - FIRST)]
        if step in TURN:
            part, token = turn(mine[TURN.index(step)], token)
            turned.append(part)
        for what, g, part in sorted(todo.get(step, ()), key=lambda item: item[0] in ("pass_over", "cross")):
            first = g * GROUP
            ks = range(first, first + GROUP)
            r, begin = chunk_of(first)
            if what == "collect":
                *given, token = gather(owner_order, token, ks, held)
                kept[g] = [lax.ppermute(x, "grp", swap) for x in given]
            elif what == "select":
                near, token = gather(owner_order, token, ks, held, kept[g])
                if r:
                    near = lax.ppermute(near, "blk", [(b, (b + r) % groups) for b in range(groups)])
                nears[g] = near
            elif what == "pass_over":
                fars[g] = lax.ppermute(nears[g], "grp", swap)
            else:
                own, count = turned[begin // FIRST], GROUP // PARTS
                out, token = cross(out, token, core_arg, own, nears[g], fars[g], r, begin, part * count, count)
    return out


def solution(mesh):
    return jax.shard_map(
        body,
        mesh=mesh,
        in_specs=(P(None, ("blk", "grp")), P()),
        out_specs=P(None, None, None, ("blk", "grp"), None),
        check_vma=False,
    )
```

profile of v0, /device:TPU:0, one launch (start us, length us, event | category | flops | bytes accessed | tf_op | source)
XLA Modules:
  0.0 277.6 jit_solution(10023846548653028356)
XLA Ops:
  0.0 3.4 %copy-done = bf16[16448,256]{1,0:T(8,128)(2,1)S(1)} copy-done((bf16[16448,256]{1,0:T(8,128)(2,1)S(1)}, bf16[16448,256]{1,0:T(8,128)(2,1)}, u32[]{:S(2)}) %copy-start) | copy-done | bytes 8421400
  4.3 5.9 %band_first.1 = (bf16[4,2,2,256,256]{4,3,2,1,0:T(8,128)(2,1)S(1)}, f32[256,256]{1,0:T(8,128)S(1)}, s32[8,128]{1,0:T(8,128)S(1)}) custom-call(s32[1]{0:T(128)} %bitcast.core_ref, bf16[16448,256]{1,0:T(8,128)(2,1)S(1)} %copy-done, bf16[16448,256]{1,0:T(8,128)(2,1)S(1)} %copy-done, bf16[256,128]{1,0:T(8,128)(2,1)S(1)} %copy-done.3), custom_call_target="tpu_custom_call" | custom-call | flops 2415919104 | bytes 12632064 | tf_op jit(solution)/shard_map/band_first/pallas_call | solution.py:119
  13.2 4.8 %collective-permute-start.8 = (bf16[2,2,256,256]{3,2,1,0:T(8,128)(2,1)S(1)}, bf16[2,2,256,256]{3,2,1,0:T(8,128)(2,1)S(1)}, u32[]{:S(2)}, u32[]{:S(2)}) collective-permute-start(bf16[2,2,256,256]{3,2,1,0:T(8,128)(2,1)S(1)} %get-tuple-element.184), channel_id=1, source_target_pairs={{0,2},{2,4},{4,6},{3,1},{5,3},{7,5},{8,10},{10,12},{12,14},{11,9},... | collective-permute-start | bytes 1572872 | tf_op jit(solution)/shard_map/ppermute | solution.py:365
  18.8 3.4 %collective-permute-start.9 = (bf16[2,2,256,256]{3,2,1,0:T(8,128)(2,1)S(1)}, bf16[2,2,256,256]{3,2,1,0:T(8,128)(2,1)S(1)}, u32[]{:S(2)}, u32[]{:S(2)}) collective-permute-start(bf16[2,2,256,256]{3,2,1,0:T(8,128)(2,1)S(1)} %get-tuple-element.186), channel_id=1, source_target_pairs={{0,2},{2,4},{4,6},{3,1},{5,3},{7,5},{8,10},{10,12},{12,14},{11,9},... | collective-permute-start | bytes 1572872 | tf_op jit(solution)/shard_map/ppermute | solution.py:365
  22.2 5.8 %band_rest.1 = (bf16[4,2,2,256,256]{4,3,2,1,0:T(8,128)(2,1)S(1)}, s32[8,128]{1,0:T(8,128)S(1)}) custom-call(s32[1]{0:T(128)} %bitcast.core_ref, bf16[16448,256]{1,0:T(8,128)(2,1)S(1)} %bitcast.18, bf16[16448,256]{1,0:T(8,128)(2,1)S(1)} %bitcast.18, bf16[256,128]{1,0:T(8,128)(2,1)S(1)} %copy-done.2, f32[256,256]{1,0:T(8,128)S(1)} %get-tuple-element.177.refs_0_, ...), custom_call_target="tpu_custom_call" | custom-call | flops 2415919104 | bytes 12632064 | tf_op jit(solution)/shard_map/band_rest/pallas_call | solution.py:119
  29.1 3.4 %collective-permute-start.10 = (bf16[2,2,256,256]{3,2,1,0:T(8,128)(2,1)S(1)}, bf16[2,2,256,256]{3,2,1,0:T(8,128)(2,1)S(1)}, u32[]{:S(2)}, u32[]{:S(2)}) collective-permute-start(bf16[2,2,256,256]{3,2,1,0:T(8,128)(2,1)S(1)} %get-tuple-element.188.refs_0_), channel_id=1, source_target_pairs={{0,2},{2,4},{4,6},{3,1},{5,3},{7,5},{8,10},{10,12},{12,14},{11,9},... | collective-permute-start | bytes 1572872 | tf_op jit(solution)/shard_map/ppermute | solution.py:365
  33.3 2.5 collective-permute-start.11
  35.9 3.2 %collective-permute-done.10.refs_6_ = bf16[2,2,256,256]{3,2,1,0:T(8,128)(2,1)S(1)} collective-permute-done((bf16[2,2,256,256]{3,2,1,0:T(8,128)(2,1)S(1)}, bf16[2,2,256,256]{3,2,1,0:T(8,128)(2,1)S(1)}, u32[]{:S(2)}, u32[]{:S(2)}) %collective-permute-start.10) | collective-permute-done | bytes 524320 | tf_op jit(solution)/shard_map/ppermute | solution.py:365
  39.9 4.3 %collective-permute-start.12 = (bf16[2,2,256,256]{3,2,1,0:T(8,128)(2,1)S(1)}, bf16[2,2,256,256]{3,2,1,0:T(8,128)(2,1)S(1)}, u32[]{:S(2)}, u32[]{:S(2)}) collective-permute-start(bf16[2,2,256,256]{3,2,1,0:T(8,128)(2,1)S(1)} %get-tuple-element.193.refs_1_), channel_id=1, source_target_pairs={{0,2},{2,4},{4,6},{3,1},{5,3},{7,5},{8,10},{10,12},{12,14},{11,9},... | collective-permute-start | bytes 1572872 | tf_op jit(solution)/shard_map/ppermute | solution.py:365
  45.5 4.3 %collective-permute-start.13 = (bf16[2,2,256,256]{3,2,1,0:T(8,128)(2,1)S(1)}, bf16[2,2,256,256]{3,2,1,0:T(8,128)(2,1)S(1)}, u32[]{:S(2)}, u32[]{:S(2)}) collective-permute-start(bf16[2,2,256,256]{3,2,1,0:T(8,128)(2,1)S(1)} %get-tuple-element.195.refs_4_), channel_id=1, source_target_pairs={{0,2},{2,4},{4,6},{3,1},{5,3},{7,5},{8,10},{10,12},{12,14},{11,9},... | collective-permute-start | bytes 1572872 | tf_op jit(solution)/shard_map/ppermute | solution.py:365
  51.7 4.3 %collective-permute-start.14 = (bf16[2,2,256,256]{3,2,1,0:T(8,128)(2,1)S(1)}, bf16[2,2,256,256]{3,2,1,0:T(8,128)(2,1)S(1)}, u32[]{:S(2)}, u32[]{:S(2)}) collective-permute-start(bf16[2,2,256,256]{3,2,1,0:T(8,128)(2,1)S(1)} %get-tuple-element.198.refs_2_.refs_0_), channel_id=1, source_target_pairs={{0,2},{2,4},{4,6},{3,1},{5,3},{7,5},{8,10},{10,12},{12,14},{11,9},... | collective-permute-start | bytes 1572872 | tf_op jit(solution)/shard_map/ppermute | solution.py:365
  57.3 4.3 %collective-permute-start.15 = (bf16[2,2,256,256]{3,2,1,0:T(8,128)(2,1)S(1)}, bf16[2,2,256,256]{3,2,1,0:T(8,128)(2,1)S(1)}, u32[]{:S(2)}, u32[]{:S(2)}) collective-permute-start(bf16[2,2,256,256]{3,2,1,0:T(8,128)(2,1)S(1)} %get-tuple-element.201.refs_5_.refs_3_), channel_id=1, source_target_pairs={{0,2},{2,4},{4,6},{3,1},{5,3},{7,5},{8,10},{10,12},{12,14},{11,9},... | collective-permute-start | bytes 1572872 | tf_op jit(solution)/shard_map/ppermute | solution.py:365
  63.5 4.3 %collective-permute-start.16 = (bf16[2,2,256,256]{3,2,1,0:T(8,128)(2,1)S(1)}, bf16[2,2,256,256]{3,2,1,0:T(8,128)(2,1)S(1)}, u32[]{:S(2)}, u32[]{:S(2)}) collective-permute-start(bf16[2,2,256,256]{3,2,1,0:T(8,128)(2,1)S(1)} %get-tuple-element.200.refs_6_.refs_1_), channel_id=1, source_target_pairs={{0,2},{2,4},{4,6},{3,1},{5,3},{7,5},{8,10},{10,12},{12,14},{11,9},... | collective-permute-start | bytes 1572872 | tf_op jit(solution)/shard_map/ppermute | solution.py:365
  69.1 4.3 %collective-permute-start.17 = (bf16[2,2,256,256]{3,2,1,0:T(8,128)(2,1)S(1)}, bf16[2,2,256,256]{3,2,1,0:T(8,128)(2,1)S(1)}, u32[]{:S(2)}, u32[]{:S(2)}) collective-permute-start(bf16[2,2,256,256]{3,2,1,0:T(8,128)(2,1)S(1)} %get-tuple-element.203.refs_7_.refs_4_), channel_id=1, source_target_pairs={{0,2},{2,4},{4,6},{3,1},{5,3},{7,5},{8,10},{10,12},{12,14},{11,9},... | collective-permute-start | bytes 1572872 | tf_op jit(solution)/shard_map/ppermute | solution.py:365
  75.2 4.3 %collective-permute-start.18 = (bf16[2,2,256,256]{3,2,1,0:T(8,128)(2,1)S(1)}, bf16[2,2,256,256]{3,2,1,0:T(8,128)(2,1)S(1)}, u32[]{:S(2)}, u32[]{:S(2)}) collective-permute-start(bf16[2,2,256,256]{3,2,1,0:T(8,128)(2,1)S(1)} %get-tuple-element.206.refs_2_.refs_0_), channel_id=1, source_target_pairs={{0,2},{2,4},{4,6},{3,1},{5,3},{7,5},{8,10},{10,12},{12,14},{11,9},... | collective-permute-start | bytes 1572872 | tf_op jit(solution)/shard_map/ppermute | solution.py:365
  80.8 4.3 %collective-permute-start.23 = (bf16[2,2,256,256]{3,2,1,0:T(8,128)(2,1)S(1)}, bf16[2,2,256,256]{3,2,1,0:T(8,128)(2,1)S(1)}, u32[]{:S(2)}, u32[]{:S(2)}) collective-permute-start(bf16[2,2,256,256]{3,2,1,0:T(8,128)(2,1)S(1)} %get-tuple-element.208.refs_5_.refs_3_), channel_id=1, source_target_pairs={{0,2},{2,4},{4,6},{3,1},{5,3},{7,5},{8,10},{10,12},{12,14},{11,9},... | collective-permute-start | bytes 1572872 | tf_op jit(solution)/shard_map/ppermute | solution.py:365
  87.0 4.3 %collective-permute-start.24 = (bf16[2,2,256,256]{3,2,1,0:T(8,128)(2,1)S(1)}, bf16[2,2,256,256]{3,2,1,0:T(8,128)(2,1)S(1)}, u32[]{:S(2)}, u32[]{:S(2)}) collective-permute-start(bf16[2,2,256,256]{3,2,1,0:T(8,128)(2,1)S(1)} %get-tuple-element.210.refs_6_.refs_1_), channel_id=1, source_target_pairs={{0,2},{2,4},{4,6},{3,1},{5,3},{7,5},{8,10},{10,12},{12,14},{11,9},... | collective-permute-start | bytes 1572872 | tf_op jit(solution)/shard_map/ppermute | solution.py:365
  94.8 2.5 collective-permute-start.25
  98.8 4.3 %collective-permute-start.26 = (bf16[2,2,256,256]{3,2,1,0:T(8,128)(2,1)S(1)}, bf16[2,2,256,256]{3,2,1,0:T(8,128)(2,1)S(1)}, u32[]{:S(2)}, u32[]{:S(2)}) collective-permute-start(bf16[2,2,256,256]{3,2,1,0:T(8,128)(2,1)S(1)} %get-tuple-element.220.refs_2_.refs_0_), channel_id=1, source_target_pairs={{0,2},{2,4},{4,6},{3,1},{5,3},{7,5},{8,10},{10,12},{12,14},{11,9},... | collective-permute-start | bytes 1572872 | tf_op jit(solution)/shard_map/ppermute | solution.py:365
  106.2 2.9 %collective-permute-start.31 = (bf16[2,2,256,256]{3,2,1,0:T(8,128)(2,1)S(1)}, bf16[2,2,256,256]{3,2,1,0:T(8,128)(2,1)S(1)}, u32[]{:S(2)}, u32[]{:S(2)}) collective-permute-start(bf16[2,2,256,256]{3,2,1,0:T(8,128)(2,1)S(1)} %get-tuple-element.224.refs_5_.refs_3_), channel_id=1, source_target_pairs={{0,2},{2,4},{4,6},{3,1},{5,3},{7,5},{8,10},{10,12},{12,14},{11,9},... | collective-permute-start | bytes 1572872 | tf_op jit(solution)/shard_map/ppermute | solution.py:365
  111.9 3.8 %collective-permute-start.32 = (bf16[2,2,256,256]{3,2,1,0:T(8,128)(2,1)S(1)}, bf16[2,2,256,256]{3,2,1,0:T(8,128)(2,1)S(1)}, u32[]{:S(2)}, u32[]{:S(2)}) collective-permute-start(bf16[2,2,256,256]{3,2,1,0:T(8,128)(2,1)S(1)} %get-tuple-element.223.refs_6_.refs_1_), channel_id=1, source_target_pairs={{0,2},{2,4},{4,6},{3,1},{5,3},{7,5},{8,10},{10,12},{12,14},{11,9},... | collective-permute-start | bytes 1572872 | tf_op jit(solution)/shard_map/ppermute | solution.py:365
  117.1 3.7 %collective-permute-start.33 = (bf16[2,2,256,256]{3,2,1,0:T(8,128)(2,1)S(1)}, bf16[2,2,256,256]{3,2,1,0:T(8,128)(2,1)S(1)}, u32[]{:S(2)}, u32[]{:S(2)}) collective-permute-start(bf16[2,2,256,256]{3,2,1,0:T(8,128)(2,1)S(1)} %get-tuple-element.231.refs_7_.refs_4_), channel_id=1, source_target_pairs={{0,2},{2,4},{4,6},{3,1},{5,3},{7,5},{8,10},{10,12},{12,14},{11,9},... | collective-permute-start | bytes 1572872 | tf_op jit(solution)/shard_map/ppermute | solution.py:365
  123.0 4.4 %collective-permute-start.34 = (bf16[2,2,256,256]{3,2,1,0:T(8,128)(2,1)S(1)}, bf16[2,2,256,256]{3,2,1,0:T(8,128)(2,1)S(1)}, u32[]{:S(2)}, u32[]{:S(2)}) collective-permute-start(bf16[2,2,256,256]{3,2,1,0:T(8,128)(2,1)S(1)} %get-tuple-element.234.refs_2_.refs_0_), channel_id=1, source_target_pairs={{0,2},{2,4},{4,6},{3,1},{5,3},{7,5},{8,10},{10,12},{12,14},{11,9},... | collective-permute-start | bytes 1572872 | tf_op jit(solution)/shard_map/ppermute | solution.py:365
  128.8 4.2 %collective-permute-start.39 = (bf16[2,2,256,256]{3,2,1,0:T(8,128)(2,1)S(1)}, bf16[2,2,256,256]{3,2,1,0:T(8,128)(2,1)S(1)}, u32[]{:S(2)}, u32[]{:S(2)}) collective-permute-start(bf16[2,2,256,256]{3,2,1,0:T(8,128)(2,1)S(1)} %get-tuple-element.236.refs_5_.refs_3_), channel_id=1, source_target_pairs={{0,2},{2,4},{4,6},{3,1},{5,3},{7,5},{8,10},{10,12},{12,14},{11,9},... | collective-permute-start | bytes 1572872 | tf_op jit(solution)/shard_map/ppermute | solution.py:365
  135.8 3.4 %collective-permute-start.40 = (bf16[2,2,256,256]{3,2,1,0:T(8,128)(2,1)S(1)}, bf16[2,2,256,256]{3,2,1,0:T(8,128)(2,1)S(1)}, u32[]{:S(2)}, u32[]{:S(2)}) collective-permute-start(bf16[2,2,256,256]{3,2,1,0:T(8,128)(2,1)S(1)} %get-tuple-element.238.refs_6_.refs_1_), channel_id=1, source_target_pairs={{0,2},{2,4},{4,6},{3,1},{5,3},{7,5},{8,10},{10,12},{12,14},{11,9},... | collective-permute-start | bytes 1572872 | tf_op jit(solution)/shard_map/ppermute | solution.py:365
  140.7 4.1 %collective-permute-start.43 = (bf16[2,2,256,256]{3,2,1,0:T(8,128)(2,1)S(1)}, bf16[2,2,256,256]{3,2,1,0:T(8,128)(2,1)S(1)}, u32[]{:S(2)}, u32[]{:S(2)}) collective-permute-start(bf16[2,2,256,256]{3,2,1,0:T(8,128)(2,1)S(1)} %get-tuple-element.245.refs_7_.refs_4_), channel_id=1, source_target_pairs={{0,2},{2,4},{4,6},{3,1},{5,3},{7,5},{8,10},{10,12},{12,14},{11,9},... | collective-permute-start | bytes 1572872 | tf_op jit(solution)/shard_map/ppermute | solution.py:365
  146.6 4.4 %collective-permute-start.44 = (bf16[2,2,256,256]{3,2,1,0:T(8,128)(2,1)S(1)}, bf16[2,2,256,256]{3,2,1,0:T(8,128)(2,1)S(1)}, u32[]{:S(2)}, u32[]{:S(2)}) collective-permute-start(bf16[2,2,256,256]{3,2,1,0:T(8,128)(2,1)S(1)} %get-tuple-element.248.refs_2_.refs_0_), channel_id=1, source_target_pairs={{0,2},{2,4},{4,6},{3,1},{5,3},{7,5},{8,10},{10,12},{12,14},{11,9},... | collective-permute-start | bytes 1572872 | tf_op jit(solution)/shard_map/ppermute | solution.py:365
  151.6 2.6 collective-permute-start.61
  157.2 2.9 %collective-permute-done.51.near_ref = bf16[4,2,256,256]{3,2,1,0:T(8,128)(2,1)S(1)} collective-permute-done((bf16[4,2,256,256]{3,2,1,0:T(8,128)(2,1)S(1)}, bf16[4,2,256,256]{3,2,1,0:T(8,128)(2,1)S(1)}, u32[]{:S(2)}, u32[]{:S(2)}) %collective-permute-start.51) | collective-permute-done | bytes 1048608 | tf_op jit(solution)/shard_map/ppermute | solution.py:385
  160.1 3.3 %collective-permute-start.49 = (bf16[2,2,256,256]{3,2,1,0:T(8,128)(2,1)S(1)}, bf16[2,2,256,256]{3,2,1,0:T(8,128)(2,1)S(1)}, u32[]{:S(2)}, u32[]{:S(2)}) collective-permute-start(bf16[2,2,256,256]{3,2,1,0:T(8,128)(2,1)S(1)} %get-tuple-element.257.refs_5_.refs_3_), channel_id=1, source_target_pairs={{0,2},{2,4},{4,6},{3,1},{5,3},{7,5},{8,10},{10,12},{12,14},{11,9},... | collective-permute-start | bytes 1572872 | tf_op jit(solution)/shard_map/ppermute | solution.py:365
  167.2 2.6 collective-permute-start.50
  171.4 3.7 %collective-permute-start.53 = (bf16[2,2,256,256]{3,2,1,0:T(8,128)(2,1)S(1)}, bf16[2,2,256,256]{3,2,1,0:T(8,128)(2,1)S(1)}, u32[]{:S(2)}, u32[]{:S(2)}) collective-permute-start(bf16[2,2,256,256]{3,2,1,0:T(8,128)(2,1)S(1)} %get-tuple-element.264.refs_7_.refs_4_), channel_id=1, source_target_pairs={{0,2},{2,4},{4,6},{3,1},{5,3},{7,5},{8,10},{10,12},{12,14},{11,9},... | collective-permute-start | bytes 1572872 | tf_op jit(solution)/shard_map/ppermute | solution.py:365
  177.3 4.3 %collective-permute-start.54 = (bf16[2,2,256,256]{3,2,1,0:T(8,128)(2,1)S(1)}, bf16[2,2,256,256]{3,2,1,0:T(8,128)(2,1)S(1)}, u32[]{:S(2)}, u32[]{:S(2)}) collective-permute-start(bf16[2,2,256,256]{3,2,1,0:T(8,128)(2,1)S(1)} %get-tuple-element.267.refs_2_.refs_0_), channel_id=1, source_target_pairs={{0,2},{2,4},{4,6},{3,1},{5,3},{7,5},{8,10},{10,12},{12,14},{11,9},... | collective-permute-start | bytes 1572872 | tf_op jit(solution)/shard_map/ppermute | solution.py:365
  187.5 3.7 %collective-permute-start.59 = (bf16[2,2,256,256]{3,2,1,0:T(8,128)(2,1)S(1)}, bf16[2,2,256,256]{3,2,1,0:T(8,128)(2,1)S(1)}, u32[]{:S(2)}, u32[]{:S(2)}) collective-permute-start(bf16[2,2,256,256]{3,2,1,0:T(8,128)(2,1)S(1)} %get-tuple-element.272.refs_5_.refs_3_), channel_id=1, source_target_pairs={{0,2},{2,4},{4,6},{3,1},{5,3},{7,5},{8,10},{10,12},{12,14},{11,9},... | collective-permute-start | bytes 1572872 | tf_op jit(solution)/shard_map/ppermute | solution.py:365
  195.0 2.7 collective-permute-start.60
  199.2 3.8 %collective-permute-start.63 = (bf16[2,2,256,256]{3,2,1,0:T(8,128)(2,1)S(1)}, bf16[2,2,256,256]{3,2,1,0:T(8,128)(2,1)S(1)}, u32[]{:S(2)}, u32[]{:S(2)}) collective-permute-start(bf16[2,2,256,256]{3,2,1,0:T(8,128)(2,1)S(1)} %get-tuple-element.283.refs_7_.refs_4_), channel_id=1, source_target_pairs={{0,2},{2,4},{4,6},{3,1},{5,3},{7,5},{8,10},{10,12},{12,14},{11,9},... | collective-permute-start | bytes 1572872 | tf_op jit(solution)/shard_map/ppermute | solution.py:365
  205.4 3.8 %collective-permute-start.64 = (bf16[2,2,256,256]{3,2,1,0:T(8,128)(2,1)S(1)}, bf16[2,2,256,256]{3,2,1,0:T(8,128)(2,1)S(1)}, u32[]{:S(2)}, u32[]{:S(2)}) collective-permute-start(bf16[2,2,256,256]{3,2,1,0:T(8,128)(2,1)S(1)} %get-tuple-element.286.refs_2_.refs_0_), channel_id=1, source_target_pairs={{0,2},{2,4},{4,6},{3,1},{5,3},{7,5},{8,10},{10,12},{12,14},{11,9},... | collective-permute-start | bytes 1572872 | tf_op jit(solution)/shard_map/ppermute | solution.py:365
  210.8 2.4 cross.20
  214.0 3.2 %collective-permute-start.69 = (bf16[2,2,256,256]{3,2,1,0:T(8,128)(2,1)S(1)}, bf16[2,2,256,256]{3,2,1,0:T(8,128)(2,1)S(1)}, u32[]{:S(2)}, u32[]{:S(2)}) collective-permute-start(bf16[2,2,256,256]{3,2,1,0:T(8,128)(2,1)S(1)} %get-tuple-element.295.refs_5_.refs_3_), channel_id=1, source_target_pairs={{0,2},{2,4},{4,6},{3,1},{5,3},{7,5},{8,10},{10,12},{12,14},{11,9},... | collective-permute-start | bytes 1572872 | tf_op jit(solution)/shard_map/ppermute | solution.py:365
  217.8 2.4 cross.21
  220.9 2.5 collective-permute-start.70
  224.8 4.2 %collective-permute-start.73 = (bf16[2,2,256,256]{3,2,1,0:T(8,128)(2,1)S(1)}, bf16[2,2,256,256]{3,2,1,0:T(8,128)(2,1)S(1)}, u32[]{:S(2)}, u32[]{:S(2)}) collective-permute-start(bf16[2,2,256,256]{3,2,1,0:T(8,128)(2,1)S(1)} %get-tuple-element.302.refs_7_.refs_4_), channel_id=1, source_target_pairs={{0,2},{2,4},{4,6},{3,1},{5,3},{7,5},{8,10},{10,12},{12,14},{11,9},... | collective-permute-start | bytes 1572872 | tf_op jit(solution)/shard_map/ppermute | solution.py:365
  230.6 4.4 %collective-permute-start.74 = (bf16[2,2,256,256]{3,2,1,0:T(8,128)(2,1)S(1)}, bf16[2,2,256,256]{3,2,1,0:T(8,128)(2,1)S(1)}, u32[]{:S(2)}, u32[]{:S(2)}) collective-permute-start(bf16[2,2,256,256]{3,2,1,0:T(8,128)(2,1)S(1)} %get-tuple-element.305.refs_2_), channel_id=1, source_target_pairs={{0,2},{2,4},{4,6},{3,1},{5,3},{7,5},{8,10},{10,12},{12,14},{11,9},... | collective-permute-start | bytes 1572872 | tf_op jit(solution)/shard_map/ppermute | solution.py:365
  239.6 3.5 %collective-permute-start.81 = (bf16[2,2,256,256]{3,2,1,0:T(8,128)(2,1)S(1)}, bf16[2,2,256,256]{3,2,1,0:T(8,128)(2,1)S(1)}, u32[]{:S(2)}, u32[]{:S(2)}) collective-permute-start(bf16[2,2,256,256]{3,2,1,0:T(8,128)(2,1)S(1)} %get-tuple-element.310.refs_5_), channel_id=1, source_target_pairs={{0,2},{2,4},{4,6},{3,1},{5,3},{7,5},{8,10},{10,12},{12,14},{11,9},... | collective-permute-start | bytes 1572872 | tf_op jit(solution)/shard_map/ppermute | solution.py:365
  247.4 2.4 cross.24
  254.7 6.0 %collective-permute-done.88.near_ref = bf16[4,2,256,256]{3,2,1,0:T(8,128)(2,1)S(1)} collective-permute-done((bf16[4,2,256,256]{3,2,1,0:T(8,128)(2,1)S(1)}, bf16[4,2,256,256]{3,2,1,0:T(8,128)(2,1)S(1)}, u32[]{:S(2)}, u32[]{:S(2)}) %collective-permute-start.88) | collective-permute-done | bytes 1048608 | tf_op jit(solution)/shard_map/ppermute | solution.py:385
  263.4 2.4 cross.26
  265.8 2.4 cross.27
  (223 shorter events, 97.8 us)
Async XLA Ops:
  11.0 17.3 %collective-permute-start.7 = (bf16[2,2,256,256]{3,2,1,0:T(8,128)(2,1)S(1)}, bf16[2,2,256,256]{3,2,1,0:T(8,128)(2,1)S(1)}, u32[]{:S(2)}, u32[]{:S(2)}) collective-permute-start(bf16[2,2,256,256]{3,2,1,0:T(8,128)(2,1)S(1)} %get-tuple-element.349), channel_id=1, source_target_pairs={{0,1},{1,0},{2,3},{3,2},{4,5},{5,4},{6,7},{7,6},{8,9},{9,8},{10,11... | collective-permute-start | bytes 1572872 | tf_op jit(solution)/shard_map/ppermute | solution.py:343
  13.2 15.2 %collective-permute-start.8 = (bf16[2,2,256,256]{3,2,1,0:T(8,128)(2,1)S(1)}, bf16[2,2,256,256]{3,2,1,0:T(8,128)(2,1)S(1)}, u32[]{:S(2)}, u32[]{:S(2)}) collective-permute-start(bf16[2,2,256,256]{3,2,1,0:T(8,128)(2,1)S(1)} %get-tuple-element.184), channel_id=1, source_target_pairs={{0,2},{2,4},{4,6},{3,1},{5,3},{7,5},{8,10},{10,12},{12,14},{11,9},... | collective-permute-start | bytes 1572872 | tf_op jit(solution)/shard_map/ppermute | solution.py:365
  18.0 14.6 %collective-permute-start.4 = (bf16[2,2,256,256]{3,2,1,0:T(8,128)(2,1)S(1)}, bf16[2,2,256,256]{3,2,1,0:T(8,128)(2,1)S(1)}, u32[]{:S(2)}, u32[]{:S(2)}) collective-permute-start(bf16[2,2,256,256]{3,2,1,0:T(8,128)(2,1)S(1)} %get-tuple-element.350), channel_id=1, source_target_pairs={{0,1},{1,0},{2,3},{3,2},{4,5},{5,4},{6,7},{7,6},{8,9},{9,8},{10,11... | collective-permute-start | bytes 1572872 | tf_op jit(solution)/shard_map/ppermute | solution.py:343
  18.8 13.8 %collective-permute-start.9 = (bf16[2,2,256,256]{3,2,1,0:T(8,128)(2,1)S(1)}, bf16[2,2,256,256]{3,2,1,0:T(8,128)(2,1)S(1)}, u32[]{:S(2)}, u32[]{:S(2)}) collective-permute-start(bf16[2,2,256,256]{3,2,1,0:T(8,128)(2,1)S(1)} %get-tuple-element.186), channel_id=1, source_target_pairs={{0,2},{2,4},{4,6},{3,1},{5,3},{7,5},{8,10},{10,12},{12,14},{11,9},... | collective-permute-start | bytes 1572872 | tf_op jit(solution)/shard_map/ppermute | solution.py:365
  32.5 11.8 %collective-permute-start.3 = (bf16[2,2,256,256]{3,2,1,0:T(8,128)(2,1)S(1)}, bf16[2,2,256,256]{3,2,1,0:T(8,128)(2,1)S(1)}, u32[]{:S(2)}, u32[]{:S(2)}) collective-permute-start(bf16[2,2,256,256]{3,2,1,0:T(8,128)(2,1)S(1)} %get-tuple-element.355), channel_id=1, source_target_pairs={{0,1},{1,0},{2,3},{3,2},{4,5},{5,4},{6,7},{7,6},{8,9},{9,8},{10,11... | collective-permute-start | bytes 1572872 | tf_op jit(solution)/shard_map/ppermute | solution.py:371
  33.3 11.4 %collective-permute-start.11 = (bf16[2,2,256,256]{3,2,1,0:T(8,128)(2,1)S(1)}, bf16[2,2,256,256]{3,2,1,0:T(8,128)(2,1)S(1)}, u32[]{:S(2)}, u32[]{:S(2)}) collective-permute-start(bf16[2,2,256,256]{3,2,1,0:T(8,128)(2,1)S(1)} %get-tuple-element.190.refs_3_), channel_id=1, source_target_pairs={{0,2},{2,4},{4,6},{3,1},{5,3},{7,5},{8,10},{10,12},{12,14},{11,9},... | collective-permute-start | bytes 1572872 | tf_op jit(solution)/shard_map/ppermute | solution.py:365
  35.8 15.1 %collective-permute-start.5 = (bf16[2,2,256,256]{3,2,1,0:T(8,128)(2,1)S(1)}, bf16[2,2,256,256]{3,2,1,0:T(8,128)(2,1)S(1)}, u32[]{:S(2)}, u32[]{:S(2)}) collective-permute-start(bf16[2,2,256,256]{3,2,1,0:T(8,128)(2,1)S(1)} %get-tuple-element.354), channel_id=1, source_target_pairs={{0,1},{1,0},{2,3},{3,2},{4,5},{5,4},{6,7},{7,6},{8,9},{9,8},{10,11... | collective-permute-start | bytes 1572872 | tf_op jit(solution)/shard_map/ppermute | solution.py:371
  39.9 11.0 %collective-permute-start.12 = (bf16[2,2,256,256]{3,2,1,0:T(8,128)(2,1)S(1)}, bf16[2,2,256,256]{3,2,1,0:T(8,128)(2,1)S(1)}, u32[]{:S(2)}, u32[]{:S(2)}) collective-permute-start(bf16[2,2,256,256]{3,2,1,0:T(8,128)(2,1)S(1)} %get-tuple-element.193.refs_1_), channel_id=1, source_target_pairs={{0,2},{2,4},{4,6},{3,1},{5,3},{7,5},{8,10},{10,12},{12,14},{11,9},... | collective-permute-start | bytes 1572872 | tf_op jit(solution)/shard_map/ppermute | solution.py:365
  44.2 11.8 %collective-permute-start.2 = (bf16[2,2,256,256]{3,2,1,0:T(8,128)(2,1)S(1)}, bf16[2,2,256,256]{3,2,1,0:T(8,128)(2,1)S(1)}, u32[]{:S(2)}, u32[]{:S(2)}) collective-permute-start(bf16[2,2,256,256]{3,2,1,0:T(8,128)(2,1)S(1)} %get-tuple-element.356), channel_id=1, source_target_pairs={{0,1},{1,0},{2,3},{3,2},{4,5},{5,4},{6,7},{7,6},{8,9},{9,8},{10,11... | collective-permute-start | bytes 1572872 | tf_op jit(solution)/shard_map/ppermute | solution.py:371
  45.5 11.0 %collective-permute-start.13 = (bf16[2,2,256,256]{3,2,1,0:T(8,128)(2,1)S(1)}, bf16[2,2,256,256]{3,2,1,0:T(8,128)(2,1)S(1)}, u32[]{:S(2)}, u32[]{:S(2)}) collective-permute-start(bf16[2,2,256,256]{3,2,1,0:T(8,128)(2,1)S(1)} %get-tuple-element.195.refs_4_), channel_id=1, source_target_pairs={{0,2},{2,4},{4,6},{3,1},{5,3},{7,5},{8,10},{10,12},{12,14},{11,9},... | collective-permute-start | bytes 1572872 | tf_op jit(solution)/shard_map/ppermute | solution.py:365
  51.7 11.0 %collective-permute-start.14 = (bf16[2,2,256,256]{3,2,1,0:T(8,128)(2,1)S(1)}, bf16[2,2,256,256]{3,2,1,0:T(8,128)(2,1)S(1)}, u32[]{:S(2)}, u32[]{:S(2)}) collective-permute-start(bf16[2,2,256,256]{3,2,1,0:T(8,128)(2,1)S(1)} %get-tuple-element.198.refs_2_.refs_0_), channel_id=1, source_target_pairs={{0,2},{2,4},{4,6},{3,1},{5,3},{7,5},{8,10},{10,12},{12,14},{11,9},... | collective-permute-start | bytes 1572872 | tf_op jit(solution)/shard_map/ppermute | solution.py:365
  57.3 11.0 %collective-permute-start.15 = (bf16[2,2,256,256]{3,2,1,0:T(8,128)(2,1)S(1)}, bf16[2,2,256,256]{3,2,1,0:T(8,128)(2,1)S(1)}, u32[]{:S(2)}, u32[]{:S(2)}) collective-permute-start(bf16[2,2,256,256]{3,2,1,0:T(8,128)(2,1)S(1)} %get-tuple-element.201.refs_5_.refs_3_), channel_id=1, source_target_pairs={{0,2},{2,4},{4,6},{3,1},{5,3},{7,5},{8,10},{10,12},{12,14},{11,9},... | collective-permute-start | bytes 1572872 | tf_op jit(solution)/shard_map/ppermute | solution.py:365
  63.5 11.0 %collective-permute-start.16 = (bf16[2,2,256,256]{3,2,1,0:T(8,128)(2,1)S(1)}, bf16[2,2,256,256]{3,2,1,0:T(8,128)(2,1)S(1)}, u32[]{:S(2)}, u32[]{:S(2)}) collective-permute-start(bf16[2,2,256,256]{3,2,1,0:T(8,128)(2,1)S(1)} %get-tuple-element.200.refs_6_.refs_1_), channel_id=1, source_target_pairs={{0,2},{2,4},{4,6},{3,1},{5,3},{7,5},{8,10},{10,12},{12,14},{11,9},... | collective-permute-start | bytes 1572872 | tf_op jit(solution)/shard_map/ppermute | solution.py:365
  69.1 11.0 %collective-permute-start.17 = (bf16[2,2,256,256]{3,2,1,0:T(8,128)(2,1)S(1)}, bf16[2,2,256,256]{3,2,1,0:T(8,128)(2,1)S(1)}, u32[]{:S(2)}, u32[]{:S(2)}) collective-permute-start(bf16[2,2,256,256]{3,2,1,0:T(8,128)(2,1)S(1)} %get-tuple-element.203.refs_7_.refs_4_), channel_id=1, source_target_pairs={{0,2},{2,4},{4,6},{3,1},{5,3},{7,5},{8,10},{10,12},{12,14},{11,9},... | collective-permute-start | bytes 1572872 | tf_op jit(solution)/shard_map/ppermute | solution.py:365
  75.2 11.0 %collective-permute-start.18 = (bf16[2,2,256,256]{3,2,1,0:T(8,128)(2,1)S(1)}, bf16[2,2,256,256]{3,2,1,0:T(8,128)(2,1)S(1)}, u32[]{:S(2)}, u32[]{:S(2)}) collective-permute-start(bf16[2,2,256,256]{3,2,1,0:T(8,128)(2,1)S(1)} %get-tuple-element.206.refs_2_.refs_0_), channel_id=1, source_target_pairs={{0,2},{2,4},{4,6},{3,1},{5,3},{7,5},{8,10},{10,12},{12,14},{11,9},... | collective-permute-start | bytes 1572872 | tf_op jit(solution)/shard_map/ppermute | solution.py:365
  79.6 11.9 %collective-permute-start.19 = (bf16[2,256,256]{2,1,0:T(8,128)(2,1)S(1)}, bf16[2,256,256]{2,1,0:T(8,128)(2,1)S(1)}, u32[]{:S(2)}, u32[]{:S(2)}) collective-permute-start(bf16[2,256,256]{2,1,0:T(8,128)(2,1)S(1)} %get-tuple-element.211), channel_id=1, source_target_pairs={{0,1},{1,0},{2,3},{3,2},{4,5},{5,4},{6,7},{7,6},{8,9},{9,8},{10,11... | collective-permute-start | bytes 786440 | tf_op jit(solution)/shard_map/ppermute | solution.py:381
  80.8 13.2 %collective-permute-start.23 = (bf16[2,2,256,256]{3,2,1,0:T(8,128)(2,1)S(1)}, bf16[2,2,256,256]{3,2,1,0:T(8,128)(2,1)S(1)}, u32[]{:S(2)}, u32[]{:S(2)}) collective-permute-start(bf16[2,2,256,256]{3,2,1,0:T(8,128)(2,1)S(1)} %get-tuple-element.208.refs_5_.refs_3_), channel_id=1, source_target_pairs={{0,2},{2,4},{4,6},{3,1},{5,3},{7,5},{8,10},{10,12},{12,14},{11,9},... | collective-permute-start | bytes 1572872 | tf_op jit(solution)/shard_map/ppermute | solution.py:365
  87.0 11.0 %collective-permute-start.24 = (bf16[2,2,256,256]{3,2,1,0:T(8,128)(2,1)S(1)}, bf16[2,2,256,256]{3,2,1,0:T(8,128)(2,1)S(1)}, u32[]{:S(2)}, u32[]{:S(2)}) collective-permute-start(bf16[2,2,256,256]{3,2,1,0:T(8,128)(2,1)S(1)} %get-tuple-element.210.refs_6_.refs_1_), channel_id=1, source_target_pairs={{0,2},{2,4},{4,6},{3,1},{5,3},{7,5},{8,10},{10,12},{12,14},{11,9},... | collective-permute-start | bytes 1572872 | tf_op jit(solution)/shard_map/ppermute | solution.py:365
  94.8 10.5 %collective-permute-start.25 = (bf16[2,2,256,256]{3,2,1,0:T(8,128)(2,1)S(1)}, bf16[2,2,256,256]{3,2,1,0:T(8,128)(2,1)S(1)}, u32[]{:S(2)}, u32[]{:S(2)}) collective-permute-start(bf16[2,2,256,256]{3,2,1,0:T(8,128)(2,1)S(1)} %get-tuple-element.217.refs_7_.refs_4_), channel_id=1, source_target_pairs={{0,2},{2,4},{4,6},{3,1},{5,3},{7,5},{8,10},{10,12},{12,14},{11,9},... | collective-permute-start | bytes 1572872 | tf_op jit(solution)/shard_map/ppermute | solution.py:365
  98.8 10.9 %collective-permute-start.26 = (bf16[2,2,256,256]{3,2,1,0:T(8,128)(2,1)S(1)}, bf16[2,2,256,256]{3,2,1,0:T(8,128)(2,1)S(1)}, u32[]{:S(2)}, u32[]{:S(2)}) collective-permute-start(bf16[2,2,256,256]{3,2,1,0:T(8,128)(2,1)S(1)} %get-tuple-element.220.refs_2_.refs_0_), channel_id=1, source_target_pairs={{0,2},{2,4},{4,6},{3,1},{5,3},{7,5},{8,10},{10,12},{12,14},{11,9},... | collective-permute-start | bytes 1572872 | tf_op jit(solution)/shard_map/ppermute | solution.py:365
  103.1 24.9 %collective-permute-start.41 = (bf16[4,2,256,256]{3,2,1,0:T(8,128)(2,1)S(1)}, bf16[4,2,256,256]{3,2,1,0:T(8,128)(2,1)S(1)}, u32[]{:S(2)}, u32[]{:S(2)}) collective-permute-start(bf16[4,2,256,256]{3,2,1,0:T(8,128)(2,1)S(1)} %get-tuple-element.250), channel_id=1, source_target_pairs={{0,8},{8,16},{16,24},{24,0},{1,9},{9,17},{17,25},{25,1},{2,10},{10... | collective-permute-start | bytes 3145736 | tf_op jit(solution)/shard_map/ppermute | solution.py:385
  117.1 11.0 %collective-permute-start.33 = (bf16[2,2,256,256]{3,2,1,0:T(8,128)(2,1)S(1)}, bf16[2,2,256,256]{3,2,1,0:T(8,128)(2,1)S(1)}, u32[]{:S(2)}, u32[]{:S(2)}) collective-permute-start(bf16[2,2,256,256]{3,2,1,0:T(8,128)(2,1)S(1)} %get-tuple-element.231.refs_7_.refs_4_), channel_id=1, source_target_pairs={{0,2},{2,4},{4,6},{3,1},{5,3},{7,5},{8,10},{10,12},{12,14},{11,9},... | collective-permute-start | bytes 1572872 | tf_op jit(solution)/shard_map/ppermute | solution.py:365
  123.0 12.0 %collective-permute-start.34 = (bf16[2,2,256,256]{3,2,1,0:T(8,128)(2,1)S(1)}, bf16[2,2,256,256]{3,2,1,0:T(8,128)(2,1)S(1)}, u32[]{:S(2)}, u32[]{:S(2)}) collective-permute-start(bf16[2,2,256,256]{3,2,1,0:T(8,128)(2,1)S(1)} %get-tuple-element.234.refs_2_.refs_0_), channel_id=1, source_target_pairs={{0,2},{2,4},{4,6},{3,1},{5,3},{7,5},{8,10},{10,12},{12,14},{11,9},... | collective-permute-start | bytes 1572872 | tf_op jit(solution)/shard_map/ppermute | solution.py:365
  128.0 23.1 %collective-permute-start.42 = (bf16[4,2,256,256]{3,2,1,0:T(8,128)(2,1)S(1)}, bf16[4,2,256,256]{3,2,1,0:T(8,128)(2,1)S(1)}, u32[]{:S(2)}, u32[]{:S(2)}) collective-permute-start(bf16[4,2,256,256]{3,2,1,0:T(8,128)(2,1)S(1)} %collective-permute-done.41.near_ref), channel_id=1, source_target_pairs={{0,1},{1,0},{2,3},{3,2},{4,5},{5,4},{6,7},{7,6},{8,9},{9,8},{10,11... | collective-permute-start | bytes 3145736 | tf_op jit(solution)/shard_map/ppermute | solution.py:388
  128.8 11.2 %collective-permute-start.39 = (bf16[2,2,256,256]{3,2,1,0:T(8,128)(2,1)S(1)}, bf16[2,2,256,256]{3,2,1,0:T(8,128)(2,1)S(1)}, u32[]{:S(2)}, u32[]{:S(2)}) collective-permute-start(bf16[2,2,256,256]{3,2,1,0:T(8,128)(2,1)S(1)} %get-tuple-element.236.refs_5_.refs_3_), channel_id=1, source_target_pairs={{0,2},{2,4},{4,6},{3,1},{5,3},{7,5},{8,10},{10,12},{12,14},{11,9},... | collective-permute-start | bytes 1572872 | tf_op jit(solution)/shard_map/ppermute | solution.py:365
  133.1 26.9 %collective-permute-start.51 = (bf16[4,2,256,256]{3,2,1,0:T(8,128)(2,1)S(1)}, bf16[4,2,256,256]{3,2,1,0:T(8,128)(2,1)S(1)}, u32[]{:S(2)}, u32[]{:S(2)}) collective-permute-start(bf16[4,2,256,256]{3,2,1,0:T(8,128)(2,1)S(1)} %get-tuple-element.268), channel_id=1, source_target_pairs={{0,8},{8,16},{16,24},{24,0},{1,9},{9,17},{17,25},{25,1},{2,10},{10... | collective-permute-start | bytes 3145736 | tf_op jit(solution)/shard_map/ppermute | solution.py:385
  140.7 10.9 %collective-permute-start.43 = (bf16[2,2,256,256]{3,2,1,0:T(8,128)(2,1)S(1)}, bf16[2,2,256,256]{3,2,1,0:T(8,128)(2,1)S(1)}, u32[]{:S(2)}, u32[]{:S(2)}) collective-permute-start(bf16[2,2,256,256]{3,2,1,0:T(8,128)(2,1)S(1)} %get-tuple-element.245.refs_7_.refs_4_), channel_id=1, source_target_pairs={{0,2},{2,4},{4,6},{3,1},{5,3},{7,5},{8,10},{10,12},{12,14},{11,9},... | collective-permute-start | bytes 1572872 | tf_op jit(solution)/shard_map/ppermute | solution.py:365
  146.6 17.4 %collective-permute-start.44 = (bf16[2,2,256,256]{3,2,1,0:T(8,128)(2,1)S(1)}, bf16[2,2,256,256]{3,2,1,0:T(8,128)(2,1)S(1)}, u32[]{:S(2)}, u32[]{:S(2)}) collective-permute-start(bf16[2,2,256,256]{3,2,1,0:T(8,128)(2,1)S(1)} %get-tuple-element.248.refs_2_.refs_0_), channel_id=1, source_target_pairs={{0,2},{2,4},{4,6},{3,1},{5,3},{7,5},{8,10},{10,12},{12,14},{11,9},... | collective-permute-start | bytes 1572872 | tf_op jit(solution)/shard_map/ppermute | solution.py:365
  151.0 12.4 %collective-permute-start.45 = (bf16[2,256,256]{2,1,0:T(8,128)(2,1)S(1)}, bf16[2,256,256]{2,1,0:T(8,128)(2,1)S(1)}, u32[]{:S(2)}, u32[]{:S(2)}) collective-permute-start(bf16[2,256,256]{2,1,0:T(8,128)(2,1)S(1)} %get-tuple-element.258), channel_id=1, source_target_pairs={{0,1},{1,0},{2,3},{3,2},{4,5},{5,4},{6,7},{7,6},{8,9},{9,8},{10,11... | collective-permute-start | bytes 786440 | tf_op jit(solution)/shard_map/ppermute | solution.py:381
  151.1 12.4 %collective-permute-start.46 = (bf16[2,256,256]{2,1,0:T(8,128)(2,1)S(1)}, bf16[2,256,256]{2,1,0:T(8,128)(2,1)S(1)}, u32[]{:S(2)}, u32[]{:S(2)}) collective-permute-start(bf16[2,256,256]{2,1,0:T(8,128)(2,1)S(1)} %get-tuple-element.259), channel_id=1, source_target_pairs={{0,1},{1,0},{2,3},{3,2},{4,5},{5,4},{6,7},{7,6},{8,9},{9,8},{10,11... | collective-permute-start | bytes 786440 | tf_op jit(solution)/shard_map/ppermute | solution.py:381
  151.6 30.5 %collective-permute-start.61 = (bf16[4,2,256,256]{3,2,1,0:T(8,128)(2,1)S(1)}, bf16[4,2,256,256]{3,2,1,0:T(8,128)(2,1)S(1)}, u32[]{:S(2)}, u32[]{:S(2)}) collective-permute-start(bf16[4,2,256,256]{3,2,1,0:T(8,128)(2,1)S(1)} %get-tuple-element.287), channel_id=1, source_target_pairs={{0,24},{8,0},{16,8},{24,16},{1,25},{9,1},{17,9},{25,17},{2,26},{10... | collective-permute-start | bytes 3145736 | tf_op jit(solution)/shard_map/ppermute | solution.py:385
  160.1 10.6 %collective-permute-start.49 = (bf16[2,2,256,256]{3,2,1,0:T(8,128)(2,1)S(1)}, bf16[2,2,256,256]{3,2,1,0:T(8,128)(2,1)S(1)}, u32[]{:S(2)}, u32[]{:S(2)}) collective-permute-start(bf16[2,2,256,256]{3,2,1,0:T(8,128)(2,1)S(1)} %get-tuple-element.257.refs_5_.refs_3_), channel_id=1, source_target_pairs={{0,2},{2,4},{4,6},{3,1},{5,3},{7,5},{8,10},{10,12},{12,14},{11,9},... | collective-permute-start | bytes 1572872 | tf_op jit(solution)/shard_map/ppermute | solution.py:365
  163.4 18.8 %collective-permute-start.52 = (bf16[4,2,256,256]{3,2,1,0:T(8,128)(2,1)S(1)}, bf16[4,2,256,256]{3,2,1,0:T(8,128)(2,1)S(1)}, u32[]{:S(2)}, u32[]{:S(2)}) collective-permute-start(bf16[4,2,256,256]{3,2,1,0:T(8,128)(2,1)S(1)} %collective-permute-done.51.near_ref), channel_id=1, source_target_pairs={{0,1},{1,0},{2,3},{3,2},{4,5},{5,4},{6,7},{7,6},{8,9},{9,8},{10,11... | collective-permute-start | bytes 3145736 | tf_op jit(solution)/shard_map/ppermute | solution.py:388
  171.4 11.2 %collective-permute-start.53 = (bf16[2,2,256,256]{3,2,1,0:T(8,128)(2,1)S(1)}, bf16[2,2,256,256]{3,2,1,0:T(8,128)(2,1)S(1)}, u32[]{:S(2)}, u32[]{:S(2)}) collective-permute-start(bf16[2,2,256,256]{3,2,1,0:T(8,128)(2,1)S(1)} %get-tuple-element.264.refs_7_.refs_4_), channel_id=1, source_target_pairs={{0,2},{2,4},{4,6},{3,1},{5,3},{7,5},{8,10},{10,12},{12,14},{11,9},... | collective-permute-start | bytes 1572872 | tf_op jit(solution)/shard_map/ppermute | solution.py:365
  177.3 14.0 %collective-permute-start.54 = (bf16[2,2,256,256]{3,2,1,0:T(8,128)(2,1)S(1)}, bf16[2,2,256,256]{3,2,1,0:T(8,128)(2,1)S(1)}, u32[]{:S(2)}, u32[]{:S(2)}) collective-permute-start(bf16[2,2,256,256]{3,2,1,0:T(8,128)(2,1)S(1)} %get-tuple-element.267.refs_2_.refs_0_), channel_id=1, source_target_pairs={{0,2},{2,4},{4,6},{3,1},{5,3},{7,5},{8,10},{10,12},{12,14},{11,9},... | collective-permute-start | bytes 1572872 | tf_op jit(solution)/shard_map/ppermute | solution.py:365
  182.2 27.0 %collective-permute-start.62 = (bf16[4,2,256,256]{3,2,1,0:T(8,128)(2,1)S(1)}, bf16[4,2,256,256]{3,2,1,0:T(8,128)(2,1)S(1)}, u32[]{:S(2)}, u32[]{:S(2)}) collective-permute-start(bf16[4,2,256,256]{3,2,1,0:T(8,128)(2,1)S(1)} %collective-permute-done.61.near_ref), channel_id=1, source_target_pairs={{0,1},{1,0},{2,3},{3,2},{4,5},{5,4},{6,7},{7,6},{8,9},{9,8},{10,11... | collective-permute-start | bytes 3145736 | tf_op jit(solution)/shard_map/ppermute | solution.py:388
  182.6 26.7 %collective-permute-start.71 = (bf16[4,2,256,256]{3,2,1,0:T(8,128)(2,1)S(1)}, bf16[4,2,256,256]{3,2,1,0:T(8,128)(2,1)S(1)}, u32[]{:S(2)}, u32[]{:S(2)}) collective-permute-start(bf16[4,2,256,256]{3,2,1,0:T(8,128)(2,1)S(1)} %get-tuple-element.306), channel_id=1, source_target_pairs={{0,24},{8,0},{16,8},{24,16},{1,25},{9,1},{17,9},{25,17},{2,26},{10... | collective-permute-start | bytes 3145736 | tf_op jit(solution)/shard_map/ppermute | solution.py:385
  187.5 10.9 %collective-permute-start.59 = (bf16[2,2,256,256]{3,2,1,0:T(8,128)(2,1)S(1)}, bf16[2,2,256,256]{3,2,1,0:T(8,128)(2,1)S(1)}, u32[]{:S(2)}, u32[]{:S(2)}) collective-permute-start(bf16[2,2,256,256]{3,2,1,0:T(8,128)(2,1)S(1)} %get-tuple-element.272.refs_5_.refs_3_), channel_id=1, source_target_pairs={{0,2},{2,4},{4,6},{3,1},{5,3},{7,5},{8,10},{10,12},{12,14},{11,9},... | collective-permute-start | bytes 1572872 | tf_op jit(solution)/shard_map/ppermute | solution.py:365
  199.2 10.6 %collective-permute-start.63 = (bf16[2,2,256,256]{3,2,1,0:T(8,128)(2,1)S(1)}, bf16[2,2,256,256]{3,2,1,0:T(8,128)(2,1)S(1)}, u32[]{:S(2)}, u32[]{:S(2)}) collective-permute-start(bf16[2,2,256,256]{3,2,1,0:T(8,128)(2,1)S(1)} %get-tuple-element.283.refs_7_.refs_4_), channel_id=1, source_target_pairs={{0,2},{2,4},{4,6},{3,1},{5,3},{7,5},{8,10},{10,12},{12,14},{11,9},... | collective-permute-start | bytes 1572872 | tf_op jit(solution)/shard_map/ppermute | solution.py:365
  203.0 26.0 %collective-permute-start.75 = (bf16[4,2,256,256]{3,2,1,0:T(8,128)(2,1)S(1)}, bf16[4,2,256,256]{3,2,1,0:T(8,128)(2,1)S(1)}, u32[]{:S(2)}, u32[]{:S(2)}) collective-permute-start(bf16[4,2,256,256]{3,2,1,0:T(8,128)(2,1)S(1)} %get-tuple-element.315), channel_id=1, source_target_pairs={{0,16},{8,24},{16,0},{24,8},{1,17},{9,25},{17,1},{25,9},{2,18},{10... | collective-permute-start | bytes 3145736 | tf_op jit(solution)/shard_map/ppermute | solution.py:385
  205.4 11.9 %collective-permute-start.64 = (bf16[2,2,256,256]{3,2,1,0:T(8,128)(2,1)S(1)}, bf16[2,2,256,256]{3,2,1,0:T(8,128)(2,1)S(1)}, u32[]{:S(2)}, u32[]{:S(2)}) collective-permute-start(bf16[2,2,256,256]{3,2,1,0:T(8,128)(2,1)S(1)} %get-tuple-element.286.refs_2_.refs_0_), channel_id=1, source_target_pairs={{0,2},{2,4},{4,6},{3,1},{5,3},{7,5},{8,10},{10,12},{12,14},{11,9},... | collective-permute-start | bytes 1572872 | tf_op jit(solution)/shard_map/ppermute | solution.py:365
  209.8 25.4 %collective-permute-start.72 = (bf16[4,2,256,256]{3,2,1,0:T(8,128)(2,1)S(1)}, bf16[4,2,256,256]{3,2,1,0:T(8,128)(2,1)S(1)}, u32[]{:S(2)}, u32[]{:S(2)}) collective-permute-start(bf16[4,2,256,256]{3,2,1,0:T(8,128)(2,1)S(1)} %collective-permute-done.71.near_ref), channel_id=1, source_target_pairs={{0,1},{1,0},{2,3},{3,2},{4,5},{5,4},{6,7},{7,6},{8,9},{9,8},{10,11... | collective-permute-start | bytes 3145736 | tf_op jit(solution)/shard_map/ppermute | solution.py:388
  224.8 11.4 %collective-permute-start.73 = (bf16[2,2,256,256]{3,2,1,0:T(8,128)(2,1)S(1)}, bf16[2,2,256,256]{3,2,1,0:T(8,128)(2,1)S(1)}, u32[]{:S(2)}, u32[]{:S(2)}) collective-permute-start(bf16[2,2,256,256]{3,2,1,0:T(8,128)(2,1)S(1)} %get-tuple-element.302.refs_7_.refs_4_), channel_id=1, source_target_pairs={{0,2},{2,4},{4,6},{3,1},{5,3},{7,5},{8,10},{10,12},{12,14},{11,9},... | collective-permute-start | bytes 1572872 | tf_op jit(solution)/shard_map/ppermute | solution.py:365
  229.0 18.5 %collective-permute-start.76 = (bf16[4,2,256,256]{3,2,1,0:T(8,128)(2,1)S(1)}, bf16[4,2,256,256]{3,2,1,0:T(8,128)(2,1)S(1)}, u32[]{:S(2)}, u32[]{:S(2)}) collective-permute-start(bf16[4,2,256,256]{3,2,1,0:T(8,128)(2,1)S(1)} %collective-permute-done.75.near_ref), channel_id=1, source_target_pairs={{0,1},{1,0},{2,3},{3,2},{4,5},{5,4},{6,7},{7,6},{8,9},{9,8},{10,11... | collective-permute-start | bytes 3145736 | tf_op jit(solution)/shard_map/ppermute | solution.py:388
  230.6 12.5 %collective-permute-start.74 = (bf16[2,2,256,256]{3,2,1,0:T(8,128)(2,1)S(1)}, bf16[2,2,256,256]{3,2,1,0:T(8,128)(2,1)S(1)}, u32[]{:S(2)}, u32[]{:S(2)}) collective-permute-start(bf16[2,2,256,256]{3,2,1,0:T(8,128)(2,1)S(1)} %get-tuple-element.305.refs_2_), channel_id=1, source_target_pairs={{0,2},{2,4},{4,6},{3,1},{5,3},{7,5},{8,10},{10,12},{12,14},{11,9},... | collective-permute-start | bytes 1572872 | tf_op jit(solution)/shard_map/ppermute | solution.py:365
  235.2 25.6 %collective-permute-start.88 = (bf16[4,2,256,256]{3,2,1,0:T(8,128)(2,1)S(1)}, bf16[4,2,256,256]{3,2,1,0:T(8,128)(2,1)S(1)}, u32[]{:S(2)}, u32[]{:S(2)}) collective-permute-start(bf16[4,2,256,256]{3,2,1,0:T(8,128)(2,1)S(1)} %get-tuple-element.335), channel_id=1, source_target_pairs={{0,16},{8,24},{16,0},{24,8},{1,17},{9,25},{17,1},{25,9},{2,18},{10... | collective-permute-start | bytes 3145736 | tf_op jit(solution)/shard_map/ppermute | solution.py:385
  239.6 12.6 %collective-permute-start.81 = (bf16[2,2,256,256]{3,2,1,0:T(8,128)(2,1)S(1)}, bf16[2,2,256,256]{3,2,1,0:T(8,128)(2,1)S(1)}, u32[]{:S(2)}, u32[]{:S(2)}) collective-permute-start(bf16[2,2,256,256]{3,2,1,0:T(8,128)(2,1)S(1)} %get-tuple-element.310.refs_5_), channel_id=1, source_target_pairs={{0,2},{2,4},{4,6},{3,1},{5,3},{7,5},{8,10},{10,12},{12,14},{11,9},... | collective-permute-start | bytes 1572872 | tf_op jit(solution)/shard_map/ppermute | solution.py:365
  262.0 10.9 %collective-permute-start.86 = (bf16[4,2,256,256]{3,2,1,0:T(8,128)(2,1)S(1)}, bf16[4,2,256,256]{3,2,1,0:T(8,128)(2,1)S(1)}, u32[]{:S(2)}, u32[]{:S(2)}) collective-permute-start(bf16[4,2,256,256]{3,2,1,0:T(8,128)(2,1)S(1)} %get-tuple-element.333.near_ref), channel_id=1, source_target_pairs={{0,1},{1,0},{2,3},{3,2},{4,5},{5,4},{6,7},{7,6},{8,9},{9,8},{10,11... | collective-permute-start | bytes 3145736 | tf_op jit(solution)/shard_map/ppermute | solution.py:388
  (49 other events, 344.5 us)
where the time goes:
time: 279 us; the launch traced here: 278 us
  starting transfers between devices  158 us (57%)
  Pallas kernels  91.1 us (33%)
  waiting for transfers between devices  22.1 us (8%)
  local copies, waits for them, and re-layouts  4.64 us (2%)
    ppermute x36, starting transfers between devices, body(): arrived.append(lax.ppermute(sent, 'grp', flow))  137 us
    pallas_call x16, Pallas kernels, cross(): pl.pallas_call(cross_kernel, grid_spec=pltpu.PrefetchScalarGridSpec(num_s...  38 us
    pallas_call x38, Pallas kernels, inject(): pl.pallas_call(kernel, in_specs=in_specs, out_specs=[in_place()] * 2, out...  27.7 us
    pallas_call x2, Pallas kernels, band(): pl.pallas_call(functools.partial(band_kernel, first), grid=(WIN // WG,),...  11.7 us
    pallas_call x16, Pallas kernels, gather(): pl.pallas_call(kernel, in_specs=[pl.BlockSpec(memory_space=pltpu.SMEM)] +...  11.6 us
    ppermute x6, starting transfers between devices, body(): lax.ppermute(near, 'blk', [(b, (b + r) % groups) for b in range(groups)])  9.81 us
    ppermute x6, waiting for transfers between devices, body(): lax.ppermute(near, 'blk', [(b, (b + r) % groups) for b in range(groups)])  9.29 us
    ppermute x36, waiting for transfers between devices, body(): arrived.append(lax.ppermute(sent, 'grp', flow))  8.96 us
  transfers between devices with their start and end apart: 90, of which 19 were waited for; matrix products, arithmetic and copies ran while one was open for 0% of the time, Pallas kernels for 29%

commit v1 on v0

--- a/solution.py
+++ b/solution.py
@@ -285,11 +285,11 @@
             total = jnp.dot(lhs, paired, preferred_element_type=jnp.float32)
             out_ref[0, part, 0] = (total * scale).astype(jnp.bfloat16)
 
-    @pl.when(pl.program_id(1) == 0)
+    @pl.when(pl.program_id(0) == 0)
     def _():
         emit(near_ref)
 
-    @pl.when(pl.program_id(1) == 1)
+    @pl.when(pl.program_id(0) == 1)
     def _():
         emit(far_ref)
 
@@ -298,16 +298,18 @@
     channels = near.shape[-1]
     first_chunk += begin
     row = first_chunk % own.shape[0]
-    paired_spec = pl.BlockSpec((1, 2, WIN, channels), lambda i, g, c: (begin + i, 0, 0, 0))
+    block = (1, 2, WIN, channels)
+    near_spec = pl.BlockSpec(block, lambda g, i, c: (begin + jnp.where(g == 0, i, count - 1), 0, 0, 0))
+    far_spec = pl.BlockSpec(block, lambda g, i, c: (begin + jnp.where(g == 0, 0, i), 0, 0, 0))
     in_specs = [
-        pl.BlockSpec((1, 1, channels, 2 * WIN), lambda i, g, c: (row + i, (c[0] + g) % CORES, 0, 0)),
-        paired_spec,
-        paired_spec,
+        pl.BlockSpec((1, 1, channels, 2 * WIN), lambda g, i, c: (row + i, (c[0] + g) % CORES, 0, 0)),
+        near_spec,
+        far_spec,
         in_place(),
     ]
     out_spec = pl.BlockSpec(
         (1, 2, 1, channels, channels),
-        lambda i, g, c: (round_index, 0, ((c[0] + g) % CORES) * HALF + first_chunk + i, 0, 0),
+        lambda g, i, c: (round_index, 0, ((c[0] + g) % CORES) * HALF + first_chunk + i, 0, 0),
     )
     args = [core, own, near, far, token]
     aliases = {}
@@ -318,7 +320,7 @@
     return pl.pallas_call(
         cross_kernel,
         grid_spec=pltpu.PrefetchScalarGridSpec(
-            num_scalar_prefetch=1, grid=(count, CORES), in_specs=in_specs, out_specs=[out_spec, in_place()]
+            num_scalar_prefetch=1, grid=(CORES, count), in_specs=in_specs, out_specs=[out_spec, in_place()]
         ),
         out_shape=[jax.ShapeDtypeStruct((ROUNDS, 2, NB, channels, channels), jnp.bfloat16), token_shape()],
         input_output_aliases=aliases,
@@ -353,7 +355,7 @@
         pick = at + (1 if left == 0 else PICK)
         give = pick + GIVE if across else pick
         meet = at + TAIL[left] if left < 4 else give + GAP
-        plan = ((at, "collect", 0), (pick, "select", 0), (give, "pass_over", 0), *((meet + i * (left >= 4), "cross", i) for i in range(PARTS)))
+        plan = ((at, "collect", 0), (pick, "select", 0), (give, "pass_over", 0), *((meet + i * (left >= 4), "cross", i) for i in range(PARTS if left >= 4 else 1)))
         for wait, what, part in plan:
             todo.setdefault(wait, []).append((what, g, part))
 
@@ -387,7 +389,7 @@
             elif what == "pass_over":
                 fars[g] = lax.ppermute(nears[g], "grp", swap)
             else:
-                own, count = turned[begin // FIRST], GROUP // PARTS
+                own, count = turned[begin // FIRST], GROUP // (PARTS if g < chunks // GROUP - 4 else 1)
                 out, token = cross(out, token, core_arg, own, nears[g], fars[g], r, begin, part * count, count)
     return out
 

time: 279 us -> 278 us (level)
  Pallas kernels: 91.1 us -> 87.9 us
    pallas_call x16 -> x12, Pallas kernels: 38 us -> 36.6 us  [cross(): pl.pallas_call(cross_kernel, grid_spec=pltpu.PrefetchScalarGridSpec(num_s...]
  transfers between devices with their start and end apart: 90 -> 90, of which waited for: 19 -> 21; matrix products, arithmetic and copies ran while one was open for 0% -> 0% of each run, Pallas kernels for 29% -> 28%
where the time goes in v1:
time: 278 us; the launch traced here: 276 us
  starting transfers between devices  159 us (57%)
  Pallas kernels  87.9 us (32%)
  waiting for transfers between devices  23 us (8%)
  local copies, waits for them, and re-layouts  4.61 us (2%)
    ppermute x36, starting transfers between devices, body(): arrived.append(lax.ppermute(sent, 'grp', flow))  139 us
    pallas_call x12, Pallas kernels, cross(): pl.pallas_call(cross_kernel, grid_spec=pltpu.PrefetchScalarGridSpec(num_s...  36.6 us
    pallas_call x38, Pallas kernels, inject(): pl.pallas_call(kernel, in_specs=in_specs, out_specs=[in_place()] * 2, out...  25.9 us
    pallas_call x2, Pallas kernels, band(): pl.pallas_call(functools.partial(band_kernel, first), grid=(WIN // WG,),...  11.7 us
    pallas_call x16, Pallas kernels, gather(): pl.pallas_call(kernel, in_specs=[pl.BlockSpec(memory_space=pltpu.SMEM)] +...  11.6 us
    ppermute x36, waiting for transfers between devices, body(): arrived.append(lax.ppermute(sent, 'grp', flow))  9.62 us
    ppermute x6, waiting for transfers between devices, body(): lax.ppermute(near, 'blk', [(b, (b + r) % groups) for b in range(groups)])  9.53 us
    ppermute x6, starting transfers between devices, body(): lax.ppermute(near, 'blk', [(b, (b + r) % groups) for b in range(groups)])  8.5 us
  transfers between devices with their start and end apart: 90, of which 21 were waited for; matrix products, arithmetic and copies ran while one was open for 0% of the time, Pallas kernels for 28%

profile of v1, /device:TPU:0, one launch (start us, length us, event | category | flops | bytes accessed | tf_op | source)
XLA Modules:
  0.0 276.4 jit_solution(531205735137365185)
XLA Ops:
  0.0 3.4 %copy-done = bf16[16448,256]{1,0:T(8,128)(2,1)S(1)} copy-done((bf16[16448,256]{1,0:T(8,128)(2,1)S(1)}, bf16[16448,256]{1,0:T(8,128)(2,1)}, u32[]{:S(2)}) %copy-start) | copy-done | bytes 8421400
  4.3 5.9 %band_first.1 = (bf16[4,2,2,256,256]{4,3,2,1,0:T(8,128)(2,1)S(1)}, f32[256,256]{1,0:T(8,128)S(1)}, s32[8,128]{1,0:T(8,128)S(1)}) custom-call(s32[1]{0:T(128)} %bitcast.core_ref, bf16[16448,256]{1,0:T(8,128)(2,1)S(1)} %copy-done, bf16[16448,256]{1,0:T(8,128)(2,1)S(1)} %copy-done, bf16[256,128]{1,0:T(8,128)(2,1)S(1)} %copy-done.3), custom_call_target="tpu_custom_call" | custom-call | flops 2415919104 | bytes 12632064 | tf_op jit(solution)/shard_map/band_first/pallas_call | solution.py:119
  13.1 4.9 %collective-permute-start.8 = (bf16[2,2,256,256]{3,2,1,0:T(8,128)(2,1)S(1)}, bf16[2,2,256,256]{3,2,1,0:T(8,128)(2,1)S(1)}, u32[]{:S(2)}, u32[]{:S(2)}) collective-permute-start(bf16[2,2,256,256]{3,2,1,0:T(8,128)(2,1)S(1)} %get-tuple-element.176), channel_id=1, source_target_pairs={{0,2},{2,4},{4,6},{3,1},{5,3},{7,5},{8,10},{10,12},{12,14},{11,9},... | collective-permute-start | bytes 1572872 | tf_op jit(solution)/shard_map/ppermute | solution.py:367
  18.7 3.5 %collective-permute-start.9 = (bf16[2,2,256,256]{3,2,1,0:T(8,128)(2,1)S(1)}, bf16[2,2,256,256]{3,2,1,0:T(8,128)(2,1)S(1)}, u32[]{:S(2)}, u32[]{:S(2)}) collective-permute-start(bf16[2,2,256,256]{3,2,1,0:T(8,128)(2,1)S(1)} %get-tuple-element.178), channel_id=1, source_target_pairs={{0,2},{2,4},{4,6},{3,1},{5,3},{7,5},{8,10},{10,12},{12,14},{11,9},... | collective-permute-start | bytes 1572872 | tf_op jit(solution)/shard_map/ppermute | solution.py:367
  22.2 5.8 %band_rest.1 = (bf16[4,2,2,256,256]{4,3,2,1,0:T(8,128)(2,1)S(1)}, s32[8,128]{1,0:T(8,128)S(1)}) custom-call(s32[1]{0:T(128)} %bitcast.core_ref, bf16[16448,256]{1,0:T(8,128)(2,1)S(1)} %bitcast.18, bf16[16448,256]{1,0:T(8,128)(2,1)S(1)} %bitcast.18, bf16[256,128]{1,0:T(8,128)(2,1)S(1)} %copy-done.2, f32[256,256]{1,0:T(8,128)S(1)} %get-tuple-element.169.refs_0_, ...), custom_call_target="tpu_custom_call" | custom-call | flops 2415919104 | bytes 12632064 | tf_op jit(solution)/shard_map/band_rest/pallas_call | solution.py:119
  29.0 3.6 %collective-permute-start.10 = (bf16[2,2,256,256]{3,2,1,0:T(8,128)(2,1)S(1)}, bf16[2,2,256,256]{3,2,1,0:T(8,128)(2,1)S(1)}, u32[]{:S(2)}, u32[]{:S(2)}) collective-permute-start(bf16[2,2,256,256]{3,2,1,0:T(8,128)(2,1)S(1)} %get-tuple-element.180.refs_0_), channel_id=1, source_target_pairs={{0,2},{2,4},{4,6},{3,1},{5,3},{7,5},{8,10},{10,12},{12,14},{11,9},... | collective-permute-start | bytes 1572872 | tf_op jit(solution)/shard_map/ppermute | solution.py:367
  33.3 2.5 collective-permute-start.11
  35.9 3.2 %collective-permute-done.10.refs_6_ = bf16[2,2,256,256]{3,2,1,0:T(8,128)(2,1)S(1)} collective-permute-done((bf16[2,2,256,256]{3,2,1,0:T(8,128)(2,1)S(1)}, bf16[2,2,256,256]{3,2,1,0:T(8,128)(2,1)S(1)}, u32[]{:S(2)}, u32[]{:S(2)}) %collective-permute-start.10) | collective-permute-done | bytes 524320 | tf_op jit(solution)/shard_map/ppermute | solution.py:367
  39.9 4.5 %collective-permute-start.12 = (bf16[2,2,256,256]{3,2,1,0:T(8,128)(2,1)S(1)}, bf16[2,2,256,256]{3,2,1,0:T(8,128)(2,1)S(1)}, u32[]{:S(2)}, u32[]{:S(2)}) collective-permute-start(bf16[2,2,256,256]{3,2,1,0:T(8,128)(2,1)S(1)} %get-tuple-element.185.refs_1_), channel_id=1, source_target_pairs={{0,2},{2,4},{4,6},{3,1},{5,3},{7,5},{8,10},{10,12},{12,14},{11,9},... | collective-permute-start | bytes 1572872 | tf_op jit(solution)/shard_map/ppermute | solution.py:367
  45.5 4.5 %collective-permute-start.13 = (bf16[2,2,256,256]{3,2,1,0:T(8,128)(2,1)S(1)}, bf16[2,2,256,256]{3,2,1,0:T(8,128)(2,1)S(1)}, u32[]{:S(2)}, u32[]{:S(2)}) collective-permute-start(bf16[2,2,256,256]{3,2,1,0:T(8,128)(2,1)S(1)} %get-tuple-element.187.refs_4_), channel_id=1, source_target_pairs={{0,2},{2,4},{4,6},{3,1},{5,3},{7,5},{8,10},{10,12},{12,14},{11,9},... | collective-permute-start | bytes 1572872 | tf_op jit(solution)/shard_map/ppermute | solution.py:367
  51.8 4.4 %collective-permute-start.14 = (bf16[2,2,256,256]{3,2,1,0:T(8,128)(2,1)S(1)}, bf16[2,2,256,256]{3,2,1,0:T(8,128)(2,1)S(1)}, u32[]{:S(2)}, u32[]{:S(2)}) collective-permute-start(bf16[2,2,256,256]{3,2,1,0:T(8,128)(2,1)S(1)} %get-tuple-element.190.refs_2_.refs_0_), channel_id=1, source_target_pairs={{0,2},{2,4},{4,6},{3,1},{5,3},{7,5},{8,10},{10,12},{12,14},{11,9},... | collective-permute-start | bytes 1572872 | tf_op jit(solution)/shard_map/ppermute | solution.py:367
  57.3 4.5 %collective-permute-start.15 = (bf16[2,2,256,256]{3,2,1,0:T(8,128)(2,1)S(1)}, bf16[2,2,256,256]{3,2,1,0:T(8,128)(2,1)S(1)}, u32[]{:S(2)}, u32[]{:S(2)}) collective-permute-start(bf16[2,2,256,256]{3,2,1,0:T(8,128)(2,1)S(1)} %get-tuple-element.193.refs_5_.refs_3_), channel_id=1, source_target_pairs={{0,2},{2,4},{4,6},{3,1},{5,3},{7,5},{8,10},{10,12},{12,14},{11,9},... | collective-permute-start | bytes 1572872 | tf_op jit(solution)/shard_map/ppermute | solution.py:367
  63.6 4.5 %collective-permute-start.16 = (bf16[2,2,256,256]{3,2,1,0:T(8,128)(2,1)S(1)}, bf16[2,2,256,256]{3,2,1,0:T(8,128)(2,1)S(1)}, u32[]{:S(2)}, u32[]{:S(2)}) collective-permute-start(bf16[2,2,256,256]{3,2,1,0:T(8,128)(2,1)S(1)} %get-tuple-element.192.refs_6_.refs_1_), channel_id=1, source_target_pairs={{0,2},{2,4},{4,6},{3,1},{5,3},{7,5},{8,10},{10,12},{12,14},{11,9},... | collective-permute-start | bytes 1572872 | tf_op jit(solution)/shard_map/ppermute | solution.py:367
  69.2 4.5 %collective-permute-start.17 = (bf16[2,2,256,256]{3,2,1,0:T(8,128)(2,1)S(1)}, bf16[2,2,256,256]{3,2,1,0:T(8,128)(2,1)S(1)}, u32[]{:S(2)}, u32[]{:S(2)}) collective-permute-start(bf16[2,2,256,256]{3,2,1,0:T(8,128)(2,1)S(1)} %get-tuple-element.195.refs_7_.refs_4_), channel_id=1, source_target_pairs={{0,2},{2,4},{4,6},{3,1},{5,3},{7,5},{8,10},{10,12},{12,14},{11,9},... | collective-permute-start | bytes 1572872 | tf_op jit(solution)/shard_map/ppermute | solution.py:367
  75.4 4.4 %collective-permute-start.18 = (bf16[2,2,256,256]{3,2,1,0:T(8,128)(2,1)S(1)}, bf16[2,2,256,256]{3,2,1,0:T(8,128)(2,1)S(1)}, u32[]{:S(2)}, u32[]{:S(2)}) collective-permute-start(bf16[2,2,256,256]{3,2,1,0:T(8,128)(2,1)S(1)} %get-tuple-element.198.refs_2_.refs_0_), channel_id=1, source_target_pairs={{0,2},{2,4},{4,6},{3,1},{5,3},{7,5},{8,10},{10,12},{12,14},{11,9},... | collective-permute-start | bytes 1572872 | tf_op jit(solution)/shard_map/ppermute | solution.py:367
  81.0 4.4 %collective-permute-start.23 = (bf16[2,2,256,256]{3,2,1,0:T(8,128)(2,1)S(1)}, bf16[2,2,256,256]{3,2,1,0:T(8,128)(2,1)S(1)}, u32[]{:S(2)}, u32[]{:S(2)}) collective-permute-start(bf16[2,2,256,256]{3,2,1,0:T(8,128)(2,1)S(1)} %get-tuple-element.200.refs_5_.refs_3_), channel_id=1, source_target_pairs={{0,2},{2,4},{4,6},{3,1},{5,3},{7,5},{8,10},{10,12},{12,14},{11,9},... | collective-permute-start | bytes 1572872 | tf_op jit(solution)/shard_map/ppermute | solution.py:367
  87.2 4.4 %collective-permute-start.24 = (bf16[2,2,256,256]{3,2,1,0:T(8,128)(2,1)S(1)}, bf16[2,2,256,256]{3,2,1,0:T(8,128)(2,1)S(1)}, u32[]{:S(2)}, u32[]{:S(2)}) collective-permute-start(bf16[2,2,256,256]{3,2,1,0:T(8,128)(2,1)S(1)} %get-tuple-element.202.refs_6_.refs_1_), channel_id=1, source_target_pairs={{0,2},{2,4},{4,6},{3,1},{5,3},{7,5},{8,10},{10,12},{12,14},{11,9},... | collective-permute-start | bytes 1572872 | tf_op jit(solution)/shard_map/ppermute | solution.py:367
  99.0 4.4 %collective-permute-start.26 = (bf16[2,2,256,256]{3,2,1,0:T(8,128)(2,1)S(1)}, bf16[2,2,256,256]{3,2,1,0:T(8,128)(2,1)S(1)}, u32[]{:S(2)}, u32[]{:S(2)}) collective-permute-start(bf16[2,2,256,256]{3,2,1,0:T(8,128)(2,1)S(1)} %get-tuple-element.212.refs_2_.refs_0_), channel_id=1, source_target_pairs={{0,2},{2,4},{4,6},{3,1},{5,3},{7,5},{8,10},{10,12},{12,14},{11,9},... | collective-permute-start | bytes 1572872 | tf_op jit(solution)/shard_map/ppermute | solution.py:367
  105.8 3.2 %collective-permute-start.31 = (bf16[2,2,256,256]{3,2,1,0:T(8,128)(2,1)S(1)}, bf16[2,2,256,256]{3,2,1,0:T(8,128)(2,1)S(1)}, u32[]{:S(2)}, u32[]{:S(2)}) collective-permute-start(bf16[2,2,256,256]{3,2,1,0:T(8,128)(2,1)S(1)} %get-tuple-element.216.refs_5_.refs_3_), channel_id=1, source_target_pairs={{0,2},{2,4},{4,6},{3,1},{5,3},{7,5},{8,10},{10,12},{12,14},{11,9},... | collective-permute-start | bytes 1572872 | tf_op jit(solution)/shard_map/ppermute | solution.py:367
  112.0 3.9 %collective-permute-start.32 = (bf16[2,2,256,256]{3,2,1,0:T(8,128)(2,1)S(1)}, bf16[2,2,256,256]{3,2,1,0:T(8,128)(2,1)S(1)}, u32[]{:S(2)}, u32[]{:S(2)}) collective-permute-start(bf16[2,2,256,256]{3,2,1,0:T(8,128)(2,1)S(1)} %get-tuple-element.215.refs_6_.refs_1_), channel_id=1, source_target_pairs={{0,2},{2,4},{4,6},{3,1},{5,3},{7,5},{8,10},{10,12},{12,14},{11,9},... | collective-permute-start | bytes 1572872 | tf_op jit(solution)/shard_map/ppermute | solution.py:367
  117.4 3.4 %collective-permute-start.33 = (bf16[2,2,256,256]{3,2,1,0:T(8,128)(2,1)S(1)}, bf16[2,2,256,256]{3,2,1,0:T(8,128)(2,1)S(1)}, u32[]{:S(2)}, u32[]{:S(2)}) collective-permute-start(bf16[2,2,256,256]{3,2,1,0:T(8,128)(2,1)S(1)} %get-tuple-element.223.refs_7_.refs_4_), channel_id=1, source_target_pairs={{0,2},{2,4},{4,6},{3,1},{5,3},{7,5},{8,10},{10,12},{12,14},{11,9},... | collective-permute-start | bytes 1572872 | tf_op jit(solution)/shard_map/ppermute | solution.py:367
  123.3 4.5 %collective-permute-start.34 = (bf16[2,2,256,256]{3,2,1,0:T(8,128)(2,1)S(1)}, bf16[2,2,256,256]{3,2,1,0:T(8,128)(2,1)S(1)}, u32[]{:S(2)}, u32[]{:S(2)}) collective-permute-start(bf16[2,2,256,256]{3,2,1,0:T(8,128)(2,1)S(1)} %get-tuple-element.226.refs_2_.refs_0_), channel_id=1, source_target_pairs={{0,2},{2,4},{4,6},{3,1},{5,3},{7,5},{8,10},{10,12},{12,14},{11,9},... | collective-permute-start | bytes 1572872 | tf_op jit(solution)/shard_map/ppermute | solution.py:367
  129.1 4.2 %collective-permute-start.39 = (bf16[2,2,256,256]{3,2,1,0:T(8,128)(2,1)S(1)}, bf16[2,2,256,256]{3,2,1,0:T(8,128)(2,1)S(1)}, u32[]{:S(2)}, u32[]{:S(2)}) collective-permute-start(bf16[2,2,256,256]{3,2,1,0:T(8,128)(2,1)S(1)} %get-tuple-element.228.refs_5_.refs_3_), channel_id=1, source_target_pairs={{0,2},{2,4},{4,6},{3,1},{5,3},{7,5},{8,10},{10,12},{12,14},{11,9},... | collective-permute-start | bytes 1572872 | tf_op jit(solution)/shard_map/ppermute | solution.py:367
  135.6 4.0 %collective-permute-start.40 = (bf16[2,2,256,256]{3,2,1,0:T(8,128)(2,1)S(1)}, bf16[2,2,256,256]{3,2,1,0:T(8,128)(2,1)S(1)}, u32[]{:S(2)}, u32[]{:S(2)}) collective-permute-start(bf16[2,2,256,256]{3,2,1,0:T(8,128)(2,1)S(1)} %get-tuple-element.230.refs_6_.refs_1_), channel_id=1, source_target_pairs={{0,2},{2,4},{4,6},{3,1},{5,3},{7,5},{8,10},{10,12},{12,14},{11,9},... | collective-permute-start | bytes 1572872 | tf_op jit(solution)/shard_map/ppermute | solution.py:367
  141.1 4.1 %collective-permute-start.43 = (bf16[2,2,256,256]{3,2,1,0:T(8,128)(2,1)S(1)}, bf16[2,2,256,256]{3,2,1,0:T(8,128)(2,1)S(1)}, u32[]{:S(2)}, u32[]{:S(2)}) collective-permute-start(bf16[2,2,256,256]{3,2,1,0:T(8,128)(2,1)S(1)} %get-tuple-element.237.refs_7_.refs_4_), channel_id=1, source_target_pairs={{0,2},{2,4},{4,6},{3,1},{5,3},{7,5},{8,10},{10,12},{12,14},{11,9},... | collective-permute-start | bytes 1572872 | tf_op jit(solution)/shard_map/ppermute | solution.py:367
  147.0 4.5 %collective-permute-start.44 = (bf16[2,2,256,256]{3,2,1,0:T(8,128)(2,1)S(1)}, bf16[2,2,256,256]{3,2,1,0:T(8,128)(2,1)S(1)}, u32[]{:S(2)}, u32[]{:S(2)}) collective-permute-start(bf16[2,2,256,256]{3,2,1,0:T(8,128)(2,1)S(1)} %get-tuple-element.240.refs_2_.refs_0_), channel_id=1, source_target_pairs={{0,2},{2,4},{4,6},{3,1},{5,3},{7,5},{8,10},{10,12},{12,14},{11,9},... | collective-permute-start | bytes 1572872 | tf_op jit(solution)/shard_map/ppermute | solution.py:367
  157.3 3.1 %collective-permute-done.51.near_ref = bf16[4,2,256,256]{3,2,1,0:T(8,128)(2,1)S(1)} collective-permute-done((bf16[4,2,256,256]{3,2,1,0:T(8,128)(2,1)S(1)}, bf16[4,2,256,256]{3,2,1,0:T(8,128)(2,1)S(1)}, u32[]{:S(2)}, u32[]{:S(2)}) %collective-permute-start.51) | collective-permute-done | bytes 1048608 | tf_op jit(solution)/shard_map/ppermute | solution.py:387
  160.4 3.0 %collective-permute-start.49 = (bf16[2,2,256,256]{3,2,1,0:T(8,128)(2,1)S(1)}, bf16[2,2,256,256]{3,2,1,0:T(8,128)(2,1)S(1)}, u32[]{:S(2)}, u32[]{:S(2)}) collective-permute-start(bf16[2,2,256,256]{3,2,1,0:T(8,128)(2,1)S(1)} %get-tuple-element.249.refs_5_.refs_3_), channel_id=1, source_target_pairs={{0,2},{2,4},{4,6},{3,1},{5,3},{7,5},{8,10},{10,12},{12,14},{11,9},... | collective-permute-start | bytes 1572872 | tf_op jit(solution)/shard_map/ppermute | solution.py:367
  164.0 2.4 cross.13
  167.1 2.9 %collective-permute-start.50 = (bf16[2,2,256,256]{3,2,1,0:T(8,128)(2,1)S(1)}, bf16[2,2,256,256]{3,2,1,0:T(8,128)(2,1)S(1)}, u32[]{:S(2)}, u32[]{:S(2)}) collective-permute-start(bf16[2,2,256,256]{3,2,1,0:T(8,128)(2,1)S(1)} %get-tuple-element.248.refs_6_.refs_1_), channel_id=1, source_target_pairs={{0,2},{2,4},{4,6},{3,1},{5,3},{7,5},{8,10},{10,12},{12,14},{11,9},... | collective-permute-start | bytes 1572872 | tf_op jit(solution)/shard_map/ppermute | solution.py:367
  171.5 3.7 %collective-permute-start.53 = (bf16[2,2,256,256]{3,2,1,0:T(8,128)(2,1)S(1)}, bf16[2,2,256,256]{3,2,1,0:T(8,128)(2,1)S(1)}, u32[]{:S(2)}, u32[]{:S(2)}) collective-permute-start(bf16[2,2,256,256]{3,2,1,0:T(8,128)(2,1)S(1)} %get-tuple-element.256.refs_7_.refs_4_), channel_id=1, source_target_pairs={{0,2},{2,4},{4,6},{3,1},{5,3},{7,5},{8,10},{10,12},{12,14},{11,9},... | collective-permute-start | bytes 1572872 | tf_op jit(solution)/shard_map/ppermute | solution.py:367
  177.4 4.4 %collective-permute-start.54 = (bf16[2,2,256,256]{3,2,1,0:T(8,128)(2,1)S(1)}, bf16[2,2,256,256]{3,2,1,0:T(8,128)(2,1)S(1)}, u32[]{:S(2)}, u32[]{:S(2)}) collective-permute-start(bf16[2,2,256,256]{3,2,1,0:T(8,128)(2,1)S(1)} %get-tuple-element.259.refs_2_.refs_0_), channel_id=1, source_target_pairs={{0,2},{2,4},{4,6},{3,1},{5,3},{7,5},{8,10},{10,12},{12,14},{11,9},... | collective-permute-start | bytes 1572872 | tf_op jit(solution)/shard_map/ppermute | solution.py:367
  184.2 2.4 cross.14
  187.2 4.0 %collective-permute-start.59 = (bf16[2,2,256,256]{3,2,1,0:T(8,128)(2,1)S(1)}, bf16[2,2,256,256]{3,2,1,0:T(8,128)(2,1)S(1)}, u32[]{:S(2)}, u32[]{:S(2)}) collective-permute-start(bf16[2,2,256,256]{3,2,1,0:T(8,128)(2,1)S(1)} %get-tuple-element.264.refs_5_.refs_3_), channel_id=1, source_target_pairs={{0,2},{2,4},{4,6},{3,1},{5,3},{7,5},{8,10},{10,12},{12,14},{11,9},... | collective-permute-start | bytes 1572872 | tf_op jit(solution)/shard_map/ppermute | solution.py:367
  194.9 2.5 collective-permute-start.60
  198.9 4.1 %collective-permute-start.63 = (bf16[2,2,256,256]{3,2,1,0:T(8,128)(2,1)S(1)}, bf16[2,2,256,256]{3,2,1,0:T(8,128)(2,1)S(1)}, u32[]{:S(2)}, u32[]{:S(2)}) collective-permute-start(bf16[2,2,256,256]{3,2,1,0:T(8,128)(2,1)S(1)} %get-tuple-element.275.refs_7_.refs_4_), channel_id=1, source_target_pairs={{0,2},{2,4},{4,6},{3,1},{5,3},{7,5},{8,10},{10,12},{12,14},{11,9},... | collective-permute-start | bytes 1572872 | tf_op jit(solution)/shard_map/ppermute | solution.py:367
  205.5 3.5 %collective-permute-start.64 = (bf16[2,2,256,256]{3,2,1,0:T(8,128)(2,1)S(1)}, bf16[2,2,256,256]{3,2,1,0:T(8,128)(2,1)S(1)}, u32[]{:S(2)}, u32[]{:S(2)}) collective-permute-start(bf16[2,2,256,256]{3,2,1,0:T(8,128)(2,1)S(1)} %get-tuple-element.278.refs_2_.refs_0_), channel_id=1, source_target_pairs={{0,2},{2,4},{4,6},{3,1},{5,3},{7,5},{8,10},{10,12},{12,14},{11,9},... | collective-permute-start | bytes 1572872 | tf_op jit(solution)/shard_map/ppermute | solution.py:367
  210.8 2.4 cross.16
  213.9 3.3 %collective-permute-start.69 = (bf16[2,2,256,256]{3,2,1,0:T(8,128)(2,1)S(1)}, bf16[2,2,256,256]{3,2,1,0:T(8,128)(2,1)S(1)}, u32[]{:S(2)}, u32[]{:S(2)}) collective-permute-start(bf16[2,2,256,256]{3,2,1,0:T(8,128)(2,1)S(1)} %get-tuple-element.287.refs_5_.refs_3_), channel_id=1, source_target_pairs={{0,2},{2,4},{4,6},{3,1},{5,3},{7,5},{8,10},{10,12},{12,14},{11,9},... | collective-permute-start | bytes 1572872 | tf_op jit(solution)/shard_map/ppermute | solution.py:367
  217.8 2.4 cross.17
  224.6 4.3 %collective-permute-start.73 = (bf16[2,2,256,256]{3,2,1,0:T(8,128)(2,1)S(1)}, bf16[2,2,256,256]{3,2,1,0:T(8,128)(2,1)S(1)}, u32[]{:S(2)}, u32[]{:S(2)}) collective-permute-start(bf16[2,2,256,256]{3,2,1,0:T(8,128)(2,1)S(1)} %get-tuple-element.294.refs_7_.refs_4_), channel_id=1, source_target_pairs={{0,2},{2,4},{4,6},{3,1},{5,3},{7,5},{8,10},{10,12},{12,14},{11,9},... | collective-permute-start | bytes 1572872 | tf_op jit(solution)/shard_map/ppermute | solution.py:367
  230.5 4.4 %collective-permute-start.74 = (bf16[2,2,256,256]{3,2,1,0:T(8,128)(2,1)S(1)}, bf16[2,2,256,256]{3,2,1,0:T(8,128)(2,1)S(1)}, u32[]{:S(2)}, u32[]{:S(2)}) collective-permute-start(bf16[2,2,256,256]{3,2,1,0:T(8,128)(2,1)S(1)} %get-tuple-element.297.refs_2_), channel_id=1, source_target_pairs={{0,2},{2,4},{4,6},{3,1},{5,3},{7,5},{8,10},{10,12},{12,14},{11,9},... | collective-permute-start | bytes 1572872 | tf_op jit(solution)/shard_map/ppermute | solution.py:367
  239.5 3.5 %collective-permute-start.81 = (bf16[2,2,256,256]{3,2,1,0:T(8,128)(2,1)S(1)}, bf16[2,2,256,256]{3,2,1,0:T(8,128)(2,1)S(1)}, u32[]{:S(2)}, u32[]{:S(2)}) collective-permute-start(bf16[2,2,256,256]{3,2,1,0:T(8,128)(2,1)S(1)} %get-tuple-element.302.refs_5_), channel_id=1, source_target_pairs={{0,2},{2,4},{4,6},{3,1},{5,3},{7,5},{8,10},{10,12},{12,14},{11,9},... | collective-permute-start | bytes 1572872 | tf_op jit(solution)/shard_map/ppermute | solution.py:367
  247.4 4.4 %cross.20 = (bf16[4,2,16,256,256]{4,3,2,1,0:T(8,128)(2,1)}, s32[8,128]{1,0:T(8,128)S(1)}) custom-call(s32[1]{0:T(128)} %bitcast.core_ref, bf16[4,2,256,512]{3,2,1,0:T(8,128)(2,1)S(1)} %get-tuple-element.241.own_ref, bf16[4,2,256,256]{3,2,1,0:T(8,128)(2,1)S(1)} %collective-permute-done.75.near_ref, ...), custom_call_target="tpu_custom_call", output_to_operand_aliasing={{0}: (5, {})} | custom-call | flops 1 | bytes 1 | tf_op jit(solution)/shard_map/cross/pallas_call | solution.py:320
  254.3 6.2 %collective-permute-done.88.near_ref = bf16[4,2,256,256]{3,2,1,0:T(8,128)(2,1)S(1)} collective-permute-done((bf16[4,2,256,256]{3,2,1,0:T(8,128)(2,1)S(1)}, bf16[4,2,256,256]{3,2,1,0:T(8,128)(2,1)S(1)}, u32[]{:S(2)}, u32[]{:S(2)}) %collective-permute-start.88) | collective-permute-done | bytes 1048608 | tf_op jit(solution)/shard_map/ppermute | solution.py:387
  263.2 4.4 %cross.21 = (bf16[4,2,16,256,256]{4,3,2,1,0:T(8,128)(2,1)}, s32[8,128]{1,0:T(8,128)S(1)}) custom-call(s32[1]{0:T(128)} %bitcast.core_ref, bf16[4,2,256,512]{3,2,1,0:T(8,128)(2,1)S(1)} %get-tuple-element.189.own_ref, bf16[4,2,256,256]{3,2,1,0:T(8,128)(2,1)S(1)} %collective-permute-done.88.near_ref, ...), custom_call_target="tpu_custom_call", output_to_operand_aliasing={{0}: (5, {})} | custom-call | flops 1 | bytes 1 | tf_op jit(solution)/shard_map/cross/pallas_call | solution.py:320
  267.6 4.4 %cross.22 = (bf16[4,2,16,256,256]{4,3,2,1,0:T(8,128)(2,1)}, s32[8,128]{1,0:T(8,128)S(1)}) custom-call(s32[1]{0:T(128)} %bitcast.core_ref, bf16[4,2,256,512]{3,2,1,0:T(8,128)(2,1)S(1)} %get-tuple-element.241.own_ref, bf16[4,2,256,256]{3,2,1,0:T(8,128)(2,1)S(1)} %get-tuple-element.324.near_ref, ...), custom_call_target="tpu_custom_call", output_to_operand_aliasing={{0}: (5, {})} | custom-call | flops 1 | bytes 1 | tf_op jit(solution)/shard_map/cross/pallas_call | solution.py:320
  272.0 4.4 %cross.23 = (bf16[4,2,16,256,256]{4,3,2,1,0:T(8,128)(2,1)}, s32[8,128]{1,0:T(8,128)}) custom-call(s32[1]{0:T(128)} %bitcast.core_ref, bf16[4,2,256,512]{3,2,1,0:T(8,128)(2,1)S(1)} %get-tuple-element.189.own_ref, bf16[4,2,256,256]{3,2,1,0:T(8,128)(2,1)S(1)} %get-tuple-element.323.near_ref, ...), custom_call_target="tpu_custom_call", output_to_operand_aliasing={{0}: (5, {})} | custom-call | flops 1 | bytes 1 | tf_op jit(solution)/shard_map/cross/pallas_call | solution.py:320
  (219 shorter events, 85.6 us)
Async XLA Ops:
  11.0 17.3 %collective-permute-start.7 = (bf16[2,2,256,256]{3,2,1,0:T(8,128)(2,1)S(1)}, bf16[2,2,256,256]{3,2,1,0:T(8,128)(2,1)S(1)}, u32[]{:S(2)}, u32[]{:S(2)}) collective-permute-start(bf16[2,2,256,256]{3,2,1,0:T(8,128)(2,1)S(1)} %get-tuple-element.333), channel_id=1, source_target_pairs={{0,1},{1,0},{2,3},{3,2},{4,5},{5,4},{6,7},{7,6},{8,9},{9,8},{10,11... | collective-permute-start | bytes 1572872 | tf_op jit(solution)/shard_map/ppermute | solution.py:345
  13.1 15.2 %collective-permute-start.8 = (bf16[2,2,256,256]{3,2,1,0:T(8,128)(2,1)S(1)}, bf16[2,2,256,256]{3,2,1,0:T(8,128)(2,1)S(1)}, u32[]{:S(2)}, u32[]{:S(2)}) collective-permute-start(bf16[2,2,256,256]{3,2,1,0:T(8,128)(2,1)S(1)} %get-tuple-element.176), channel_id=1, source_target_pairs={{0,2},{2,4},{4,6},{3,1},{5,3},{7,5},{8,10},{10,12},{12,14},{11,9},... | collective-permute-start | bytes 1572872 | tf_op jit(solution)/shard_map/ppermute | solution.py:367
  18.0 14.6 %collective-permute-start.4 = (bf16[2,2,256,256]{3,2,1,0:T(8,128)(2,1)S(1)}, bf16[2,2,256,256]{3,2,1,0:T(8,128)(2,1)S(1)}, u32[]{:S(2)}, u32[]{:S(2)}) collective-permute-start(bf16[2,2,256,256]{3,2,1,0:T(8,128)(2,1)S(1)} %get-tuple-element.334), channel_id=1, source_target_pairs={{0,1},{1,0},{2,3},{3,2},{4,5},{5,4},{6,7},{7,6},{8,9},{9,8},{10,11... | collective-permute-start | bytes 1572872 | tf_op jit(solution)/shard_map/ppermute | solution.py:345
  18.7 13.9 %collective-permute-start.9 = (bf16[2,2,256,256]{3,2,1,0:T(8,128)(2,1)S(1)}, bf16[2,2,256,256]{3,2,1,0:T(8,128)(2,1)S(1)}, u32[]{:S(2)}, u32[]{:S(2)}) collective-permute-start(bf16[2,2,256,256]{3,2,1,0:T(8,128)(2,1)S(1)} %get-tuple-element.178), channel_id=1, source_target_pairs={{0,2},{2,4},{4,6},{3,1},{5,3},{7,5},{8,10},{10,12},{12,14},{11,9},... | collective-permute-start | bytes 1572872 | tf_op jit(solution)/shard_map/ppermute | solution.py:367
  32.5 11.9 %collective-permute-start.3 = (bf16[2,2,256,256]{3,2,1,0:T(8,128)(2,1)S(1)}, bf16[2,2,256,256]{3,2,1,0:T(8,128)(2,1)S(1)}, u32[]{:S(2)}, u32[]{:S(2)}) collective-permute-start(bf16[2,2,256,256]{3,2,1,0:T(8,128)(2,1)S(1)} %get-tuple-element.339), channel_id=1, source_target_pairs={{0,1},{1,0},{2,3},{3,2},{4,5},{5,4},{6,7},{7,6},{8,9},{9,8},{10,11... | collective-permute-start | bytes 1572872 | tf_op jit(solution)/shard_map/ppermute | solution.py:373
  33.3 11.5 %collective-permute-start.11 = (bf16[2,2,256,256]{3,2,1,0:T(8,128)(2,1)S(1)}, bf16[2,2,256,256]{3,2,1,0:T(8,128)(2,1)S(1)}, u32[]{:S(2)}, u32[]{:S(2)}) collective-permute-start(bf16[2,2,256,256]{3,2,1,0:T(8,128)(2,1)S(1)} %get-tuple-element.182.refs_3_), channel_id=1, source_target_pairs={{0,2},{2,4},{4,6},{3,1},{5,3},{7,5},{8,10},{10,12},{12,14},{11,9},... | collective-permute-start | bytes 1572872 | tf_op jit(solution)/shard_map/ppermute | solution.py:367
  35.8 15.2 %collective-permute-start.5 = (bf16[2,2,256,256]{3,2,1,0:T(8,128)(2,1)S(1)}, bf16[2,2,256,256]{3,2,1,0:T(8,128)(2,1)S(1)}, u32[]{:S(2)}, u32[]{:S(2)}) collective-permute-start(bf16[2,2,256,256]{3,2,1,0:T(8,128)(2,1)S(1)} %get-tuple-element.338), channel_id=1, source_target_pairs={{0,1},{1,0},{2,3},{3,2},{4,5},{5,4},{6,7},{7,6},{8,9},{9,8},{10,11... | collective-permute-start | bytes 1572872 | tf_op jit(solution)/shard_map/ppermute | solution.py:373
  39.9 11.2 %collective-permute-start.12 = (bf16[2,2,256,256]{3,2,1,0:T(8,128)(2,1)S(1)}, bf16[2,2,256,256]{3,2,1,0:T(8,128)(2,1)S(1)}, u32[]{:S(2)}, u32[]{:S(2)}) collective-permute-start(bf16[2,2,256,256]{3,2,1,0:T(8,128)(2,1)S(1)} %get-tuple-element.185.refs_1_), channel_id=1, source_target_pairs={{0,2},{2,4},{4,6},{3,1},{5,3},{7,5},{8,10},{10,12},{12,14},{11,9},... | collective-permute-start | bytes 1572872 | tf_op jit(solution)/shard_map/ppermute | solution.py:367
  44.4 11.8 %collective-permute-start.2 = (bf16[2,2,256,256]{3,2,1,0:T(8,128)(2,1)S(1)}, bf16[2,2,256,256]{3,2,1,0:T(8,128)(2,1)S(1)}, u32[]{:S(2)}, u32[]{:S(2)}) collective-permute-start(bf16[2,2,256,256]{3,2,1,0:T(8,128)(2,1)S(1)} %get-tuple-element.340), channel_id=1, source_target_pairs={{0,1},{1,0},{2,3},{3,2},{4,5},{5,4},{6,7},{7,6},{8,9},{9,8},{10,11... | collective-permute-start | bytes 1572872 | tf_op jit(solution)/shard_map/ppermute | solution.py:373
  45.5 11.1 %collective-permute-start.13 = (bf16[2,2,256,256]{3,2,1,0:T(8,128)(2,1)S(1)}, bf16[2,2,256,256]{3,2,1,0:T(8,128)(2,1)S(1)}, u32[]{:S(2)}, u32[]{:S(2)}) collective-permute-start(bf16[2,2,256,256]{3,2,1,0:T(8,128)(2,1)S(1)} %get-tuple-element.187.refs_4_), channel_id=1, source_target_pairs={{0,2},{2,4},{4,6},{3,1},{5,3},{7,5},{8,10},{10,12},{12,14},{11,9},... | collective-permute-start | bytes 1572872 | tf_op jit(solution)/shard_map/ppermute | solution.py:367
  51.8 11.1 %collective-permute-start.14 = (bf16[2,2,256,256]{3,2,1,0:T(8,128)(2,1)S(1)}, bf16[2,2,256,256]{3,2,1,0:T(8,128)(2,1)S(1)}, u32[]{:S(2)}, u32[]{:S(2)}) collective-permute-start(bf16[2,2,256,256]{3,2,1,0:T(8,128)(2,1)S(1)} %get-tuple-element.190.refs_2_.refs_0_), channel_id=1, source_target_pairs={{0,2},{2,4},{4,6},{3,1},{5,3},{7,5},{8,10},{10,12},{12,14},{11,9},... | collective-permute-start | bytes 1572872 | tf_op jit(solution)/shard_map/ppermute | solution.py:367
  57.3 11.1 %collective-permute-start.15 = (bf16[2,2,256,256]{3,2,1,0:T(8,128)(2,1)S(1)}, bf16[2,2,256,256]{3,2,1,0:T(8,128)(2,1)S(1)}, u32[]{:S(2)}, u32[]{:S(2)}) collective-permute-start(bf16[2,2,256,256]{3,2,1,0:T(8,128)(2,1)S(1)} %get-tuple-element.193.refs_5_.refs_3_), channel_id=1, source_target_pairs={{0,2},{2,4},{4,6},{3,1},{5,3},{7,5},{8,10},{10,12},{12,14},{11,9},... | collective-permute-start | bytes 1572872 | tf_op jit(solution)/shard_map/ppermute | solution.py:367
  63.6 11.1 %collective-permute-start.16 = (bf16[2,2,256,256]{3,2,1,0:T(8,128)(2,1)S(1)}, bf16[2,2,256,256]{3,2,1,0:T(8,128)(2,1)S(1)}, u32[]{:S(2)}, u32[]{:S(2)}) collective-permute-start(bf16[2,2,256,256]{3,2,1,0:T(8,128)(2,1)S(1)} %get-tuple-element.192.refs_6_.refs_1_), channel_id=1, source_target_pairs={{0,2},{2,4},{4,6},{3,1},{5,3},{7,5},{8,10},{10,12},{12,14},{11,9},... | collective-permute-start | bytes 1572872 | tf_op jit(solution)/shard_map/ppermute | solution.py:367
  69.2 11.1 %collective-permute-start.17 = (bf16[2,2,256,256]{3,2,1,0:T(8,128)(2,1)S(1)}, bf16[2,2,256,256]{3,2,1,0:T(8,128)(2,1)S(1)}, u32[]{:S(2)}, u32[]{:S(2)}) collective-permute-start(bf16[2,2,256,256]{3,2,1,0:T(8,128)(2,1)S(1)} %get-tuple-element.195.refs_7_.refs_4_), channel_id=1, source_target_pairs={{0,2},{2,4},{4,6},{3,1},{5,3},{7,5},{8,10},{10,12},{12,14},{11,9},... | collective-permute-start | bytes 1572872 | tf_op jit(solution)/shard_map/ppermute | solution.py:367
  75.4 11.1 %collective-permute-start.18 = (bf16[2,2,256,256]{3,2,1,0:T(8,128)(2,1)S(1)}, bf16[2,2,256,256]{3,2,1,0:T(8,128)(2,1)S(1)}, u32[]{:S(2)}, u32[]{:S(2)}) collective-permute-start(bf16[2,2,256,256]{3,2,1,0:T(8,128)(2,1)S(1)} %get-tuple-element.198.refs_2_.refs_0_), channel_id=1, source_target_pairs={{0,2},{2,4},{4,6},{3,1},{5,3},{7,5},{8,10},{10,12},{12,14},{11,9},... | collective-permute-start | bytes 1572872 | tf_op jit(solution)/shard_map/ppermute | solution.py:367
  79.8 11.9 %collective-permute-start.19 = (bf16[2,256,256]{2,1,0:T(8,128)(2,1)S(1)}, bf16[2,256,256]{2,1,0:T(8,128)(2,1)S(1)}, u32[]{:S(2)}, u32[]{:S(2)}) collective-permute-start(bf16[2,256,256]{2,1,0:T(8,128)(2,1)S(1)} %get-tuple-element.203), channel_id=1, source_target_pairs={{0,1},{1,0},{2,3},{3,2},{4,5},{5,4},{6,7},{7,6},{8,9},{9,8},{10,11... | collective-permute-start | bytes 786440 | tf_op jit(solution)/shard_map/ppermute | solution.py:383
  81.0 13.3 %collective-permute-start.23 = (bf16[2,2,256,256]{3,2,1,0:T(8,128)(2,1)S(1)}, bf16[2,2,256,256]{3,2,1,0:T(8,128)(2,1)S(1)}, u32[]{:S(2)}, u32[]{:S(2)}) collective-permute-start(bf16[2,2,256,256]{3,2,1,0:T(8,128)(2,1)S(1)} %get-tuple-element.200.refs_5_.refs_3_), channel_id=1, source_target_pairs={{0,2},{2,4},{4,6},{3,1},{5,3},{7,5},{8,10},{10,12},{12,14},{11,9},... | collective-permute-start | bytes 1572872 | tf_op jit(solution)/shard_map/ppermute | solution.py:367
  87.2 11.1 %collective-permute-start.24 = (bf16[2,2,256,256]{3,2,1,0:T(8,128)(2,1)S(1)}, bf16[2,2,256,256]{3,2,1,0:T(8,128)(2,1)S(1)}, u32[]{:S(2)}, u32[]{:S(2)}) collective-permute-start(bf16[2,2,256,256]{3,2,1,0:T(8,128)(2,1)S(1)} %get-tuple-element.202.refs_6_.refs_1_), channel_id=1, source_target_pairs={{0,2},{2,4},{4,6},{3,1},{5,3},{7,5},{8,10},{10,12},{12,14},{11,9},... | collective-permute-start | bytes 1572872 | tf_op jit(solution)/shard_map/ppermute | solution.py:367
  99.0 11.1 %collective-permute-start.26 = (bf16[2,2,256,256]{3,2,1,0:T(8,128)(2,1)S(1)}, bf16[2,2,256,256]{3,2,1,0:T(8,128)(2,1)S(1)}, u32[]{:S(2)}, u32[]{:S(2)}) collective-permute-start(bf16[2,2,256,256]{3,2,1,0:T(8,128)(2,1)S(1)} %get-tuple-element.212.refs_2_.refs_0_), channel_id=1, source_target_pairs={{0,2},{2,4},{4,6},{3,1},{5,3},{7,5},{8,10},{10,12},{12,14},{11,9},... | collective-permute-start | bytes 1572872 | tf_op jit(solution)/shard_map/ppermute | solution.py:367
  103.4 25.0 %collective-permute-start.41 = (bf16[4,2,256,256]{3,2,1,0:T(8,128)(2,1)S(1)}, bf16[4,2,256,256]{3,2,1,0:T(8,128)(2,1)S(1)}, u32[]{:S(2)}, u32[]{:S(2)}) collective-permute-start(bf16[4,2,256,256]{3,2,1,0:T(8,128)(2,1)S(1)} %get-tuple-element.242), channel_id=1, source_target_pairs={{0,8},{8,16},{16,24},{24,0},{1,9},{9,17},{17,25},{25,1},{2,10},{10... | collective-permute-start | bytes 3145736 | tf_op jit(solution)/shard_map/ppermute | solution.py:387
  105.8 10.9 %collective-permute-start.31 = (bf16[2,2,256,256]{3,2,1,0:T(8,128)(2,1)S(1)}, bf16[2,2,256,256]{3,2,1,0:T(8,128)(2,1)S(1)}, u32[]{:S(2)}, u32[]{:S(2)}) collective-permute-start(bf16[2,2,256,256]{3,2,1,0:T(8,128)(2,1)S(1)} %get-tuple-element.216.refs_5_.refs_3_), channel_id=1, source_target_pairs={{0,2},{2,4},{4,6},{3,1},{5,3},{7,5},{8,10},{10,12},{12,14},{11,9},... | collective-permute-start | bytes 1572872 | tf_op jit(solution)/shard_map/ppermute | solution.py:367
  112.0 10.6 %collective-permute-start.32 = (bf16[2,2,256,256]{3,2,1,0:T(8,128)(2,1)S(1)}, bf16[2,2,256,256]{3,2,1,0:T(8,128)(2,1)S(1)}, u32[]{:S(2)}, u32[]{:S(2)}) collective-permute-start(bf16[2,2,256,256]{3,2,1,0:T(8,128)(2,1)S(1)} %get-tuple-element.215.refs_6_.refs_1_), channel_id=1, source_target_pairs={{0,2},{2,4},{4,6},{3,1},{5,3},{7,5},{8,10},{10,12},{12,14},{11,9},... | collective-permute-start | bytes 1572872 | tf_op jit(solution)/shard_map/ppermute | solution.py:367
  117.4 11.0 %collective-permute-start.33 = (bf16[2,2,256,256]{3,2,1,0:T(8,128)(2,1)S(1)}, bf16[2,2,256,256]{3,2,1,0:T(8,128)(2,1)S(1)}, u32[]{:S(2)}, u32[]{:S(2)}) collective-permute-start(bf16[2,2,256,256]{3,2,1,0:T(8,128)(2,1)S(1)} %get-tuple-element.223.refs_7_.refs_4_), channel_id=1, source_target_pairs={{0,2},{2,4},{4,6},{3,1},{5,3},{7,5},{8,10},{10,12},{12,14},{11,9},... | collective-permute-start | bytes 1572872 | tf_op jit(solution)/shard_map/ppermute | solution.py:367
  123.3 11.5 %collective-permute-start.34 = (bf16[2,2,256,256]{3,2,1,0:T(8,128)(2,1)S(1)}, bf16[2,2,256,256]{3,2,1,0:T(8,128)(2,1)S(1)}, u32[]{:S(2)}, u32[]{:S(2)}) collective-permute-start(bf16[2,2,256,256]{3,2,1,0:T(8,128)(2,1)S(1)} %get-tuple-element.226.refs_2_.refs_0_), channel_id=1, source_target_pairs={{0,2},{2,4},{4,6},{3,1},{5,3},{7,5},{8,10},{10,12},{12,14},{11,9},... | collective-permute-start | bytes 1572872 | tf_op jit(solution)/shard_map/ppermute | solution.py:367
  128.3 23.2 %collective-permute-start.42 = (bf16[4,2,256,256]{3,2,1,0:T(8,128)(2,1)S(1)}, bf16[4,2,256,256]{3,2,1,0:T(8,128)(2,1)S(1)}, u32[]{:S(2)}, u32[]{:S(2)}) collective-permute-start(bf16[4,2,256,256]{3,2,1,0:T(8,128)(2,1)S(1)} %collective-permute-done.41.near_ref), channel_id=1, source_target_pairs={{0,1},{1,0},{2,3},{3,2},{4,5},{5,4},{6,7},{7,6},{8,9},{9,8},{10,11... | collective-permute-start | bytes 3145736 | tf_op jit(solution)/shard_map/ppermute | solution.py:390
  129.1 11.3 %collective-permute-start.39 = (bf16[2,2,256,256]{3,2,1,0:T(8,128)(2,1)S(1)}, bf16[2,2,256,256]{3,2,1,0:T(8,128)(2,1)S(1)}, u32[]{:S(2)}, u32[]{:S(2)}) collective-permute-start(bf16[2,2,256,256]{3,2,1,0:T(8,128)(2,1)S(1)} %get-tuple-element.228.refs_5_.refs_3_), channel_id=1, source_target_pairs={{0,2},{2,4},{4,6},{3,1},{5,3},{7,5},{8,10},{10,12},{12,14},{11,9},... | collective-permute-start | bytes 1572872 | tf_op jit(solution)/shard_map/ppermute | solution.py:367
  133.5 26.9 %collective-permute-start.51 = (bf16[4,2,256,256]{3,2,1,0:T(8,128)(2,1)S(1)}, bf16[4,2,256,256]{3,2,1,0:T(8,128)(2,1)S(1)}, u32[]{:S(2)}, u32[]{:S(2)}) collective-permute-start(bf16[4,2,256,256]{3,2,1,0:T(8,128)(2,1)S(1)} %get-tuple-element.260), channel_id=1, source_target_pairs={{0,8},{8,16},{16,24},{24,0},{1,9},{9,17},{17,25},{25,1},{2,10},{10... | collective-permute-start | bytes 3145736 | tf_op jit(solution)/shard_map/ppermute | solution.py:387
  135.6 10.6 %collective-permute-start.40 = (bf16[2,2,256,256]{3,2,1,0:T(8,128)(2,1)S(1)}, bf16[2,2,256,256]{3,2,1,0:T(8,128)(2,1)S(1)}, u32[]{:S(2)}, u32[]{:S(2)}) collective-permute-start(bf16[2,2,256,256]{3,2,1,0:T(8,128)(2,1)S(1)} %get-tuple-element.230.refs_6_.refs_1_), channel_id=1, source_target_pairs={{0,2},{2,4},{4,6},{3,1},{5,3},{7,5},{8,10},{10,12},{12,14},{11,9},... | collective-permute-start | bytes 1572872 | tf_op jit(solution)/shard_map/ppermute | solution.py:367
  141.1 11.0 %collective-permute-start.43 = (bf16[2,2,256,256]{3,2,1,0:T(8,128)(2,1)S(1)}, bf16[2,2,256,256]{3,2,1,0:T(8,128)(2,1)S(1)}, u32[]{:S(2)}, u32[]{:S(2)}) collective-permute-start(bf16[2,2,256,256]{3,2,1,0:T(8,128)(2,1)S(1)} %get-tuple-element.237.refs_7_.refs_4_), channel_id=1, source_target_pairs={{0,2},{2,4},{4,6},{3,1},{5,3},{7,5},{8,10},{10,12},{12,14},{11,9},... | collective-permute-start | bytes 1572872 | tf_op jit(solution)/shard_map/ppermute | solution.py:367
  147.0 17.0 %collective-permute-start.44 = (bf16[2,2,256,256]{3,2,1,0:T(8,128)(2,1)S(1)}, bf16[2,2,256,256]{3,2,1,0:T(8,128)(2,1)S(1)}, u32[]{:S(2)}, u32[]{:S(2)}) collective-permute-start(bf16[2,2,256,256]{3,2,1,0:T(8,128)(2,1)S(1)} %get-tuple-element.240.refs_2_.refs_0_), channel_id=1, source_target_pairs={{0,2},{2,4},{4,6},{3,1},{5,3},{7,5},{8,10},{10,12},{12,14},{11,9},... | collective-permute-start | bytes 1572872 | tf_op jit(solution)/shard_map/ppermute | solution.py:367
  151.5 11.9 %collective-permute-start.45 = (bf16[2,256,256]{2,1,0:T(8,128)(2,1)S(1)}, bf16[2,256,256]{2,1,0:T(8,128)(2,1)S(1)}, u32[]{:S(2)}, u32[]{:S(2)}) collective-permute-start(bf16[2,256,256]{2,1,0:T(8,128)(2,1)S(1)} %get-tuple-element.250), channel_id=1, source_target_pairs={{0,1},{1,0},{2,3},{3,2},{4,5},{5,4},{6,7},{7,6},{8,9},{9,8},{10,11... | collective-permute-start | bytes 786440 | tf_op jit(solution)/shard_map/ppermute | solution.py:383
  151.6 11.9 %collective-permute-start.46 = (bf16[2,256,256]{2,1,0:T(8,128)(2,1)S(1)}, bf16[2,256,256]{2,1,0:T(8,128)(2,1)S(1)}, u32[]{:S(2)}, u32[]{:S(2)}) collective-permute-start(bf16[2,256,256]{2,1,0:T(8,128)(2,1)S(1)} %get-tuple-element.251), channel_id=1, source_target_pairs={{0,1},{1,0},{2,3},{3,2},{4,5},{5,4},{6,7},{7,6},{8,9},{9,8},{10,11... | collective-permute-start | bytes 786440 | tf_op jit(solution)/shard_map/ppermute | solution.py:383
  152.1 30.0 %collective-permute-start.61 = (bf16[4,2,256,256]{3,2,1,0:T(8,128)(2,1)S(1)}, bf16[4,2,256,256]{3,2,1,0:T(8,128)(2,1)S(1)}, u32[]{:S(2)}, u32[]{:S(2)}) collective-permute-start(bf16[4,2,256,256]{3,2,1,0:T(8,128)(2,1)S(1)} %get-tuple-element.279), channel_id=1, source_target_pairs={{0,24},{8,0},{16,8},{24,16},{1,25},{9,1},{17,9},{25,17},{2,26},{10... | collective-permute-start | bytes 3145736 | tf_op jit(solution)/shard_map/ppermute | solution.py:387
  163.4 19.1 %collective-permute-start.52 = (bf16[4,2,256,256]{3,2,1,0:T(8,128)(2,1)S(1)}, bf16[4,2,256,256]{3,2,1,0:T(8,128)(2,1)S(1)}, u32[]{:S(2)}, u32[]{:S(2)}) collective-permute-start(bf16[4,2,256,256]{3,2,1,0:T(8,128)(2,1)S(1)} %collective-permute-done.51.near_ref), channel_id=1, source_target_pairs={{0,1},{1,0},{2,3},{3,2},{4,5},{5,4},{6,7},{7,6},{8,9},{9,8},{10,11... | collective-permute-start | bytes 3145736 | tf_op jit(solution)/shard_map/ppermute | solution.py:390
  171.5 11.1 %collective-permute-start.53 = (bf16[2,2,256,256]{3,2,1,0:T(8,128)(2,1)S(1)}, bf16[2,2,256,256]{3,2,1,0:T(8,128)(2,1)S(1)}, u32[]{:S(2)}, u32[]{:S(2)}) collective-permute-start(bf16[2,2,256,256]{3,2,1,0:T(8,128)(2,1)S(1)} %get-tuple-element.256.refs_7_.refs_4_), channel_id=1, source_target_pairs={{0,2},{2,4},{4,6},{3,1},{5,3},{7,5},{8,10},{10,12},{12,14},{11,9},... | collective-permute-start | bytes 1572872 | tf_op jit(solution)/shard_map/ppermute | solution.py:367
  177.4 13.9 %collective-permute-start.54 = (bf16[2,2,256,256]{3,2,1,0:T(8,128)(2,1)S(1)}, bf16[2,2,256,256]{3,2,1,0:T(8,128)(2,1)S(1)}, u32[]{:S(2)}, u32[]{:S(2)}) collective-permute-start(bf16[2,2,256,256]{3,2,1,0:T(8,128)(2,1)S(1)} %get-tuple-element.259.refs_2_.refs_0_), channel_id=1, source_target_pairs={{0,2},{2,4},{4,6},{3,1},{5,3},{7,5},{8,10},{10,12},{12,14},{11,9},... | collective-permute-start | bytes 1572872 | tf_op jit(solution)/shard_map/ppermute | solution.py:367
  182.4 26.6 %collective-permute-start.62 = (bf16[4,2,256,256]{3,2,1,0:T(8,128)(2,1)S(1)}, bf16[4,2,256,256]{3,2,1,0:T(8,128)(2,1)S(1)}, u32[]{:S(2)}, u32[]{:S(2)}) collective-permute-start(bf16[4,2,256,256]{3,2,1,0:T(8,128)(2,1)S(1)} %collective-permute-done.61.near_ref), channel_id=1, source_target_pairs={{0,1},{1,0},{2,3},{3,2},{4,5},{5,4},{6,7},{7,6},{8,9},{9,8},{10,11... | collective-permute-start | bytes 3145736 | tf_op jit(solution)/shard_map/ppermute | solution.py:390
  182.6 26.5 %collective-permute-start.71 = (bf16[4,2,256,256]{3,2,1,0:T(8,128)(2,1)S(1)}, bf16[4,2,256,256]{3,2,1,0:T(8,128)(2,1)S(1)}, u32[]{:S(2)}, u32[]{:S(2)}) collective-permute-start(bf16[4,2,256,256]{3,2,1,0:T(8,128)(2,1)S(1)} %get-tuple-element.298), channel_id=1, source_target_pairs={{0,24},{8,0},{16,8},{24,16},{1,25},{9,1},{17,9},{25,17},{2,26},{10... | collective-permute-start | bytes 3145736 | tf_op jit(solution)/shard_map/ppermute | solution.py:387
  187.2 11.0 %collective-permute-start.59 = (bf16[2,2,256,256]{3,2,1,0:T(8,128)(2,1)S(1)}, bf16[2,2,256,256]{3,2,1,0:T(8,128)(2,1)S(1)}, u32[]{:S(2)}, u32[]{:S(2)}) collective-permute-start(bf16[2,2,256,256]{3,2,1,0:T(8,128)(2,1)S(1)} %get-tuple-element.264.refs_5_.refs_3_), channel_id=1, source_target_pairs={{0,2},{2,4},{4,6},{3,1},{5,3},{7,5},{8,10},{10,12},{12,14},{11,9},... | collective-permute-start | bytes 1572872 | tf_op jit(solution)/shard_map/ppermute | solution.py:367
  198.9 10.7 %collective-permute-start.63 = (bf16[2,2,256,256]{3,2,1,0:T(8,128)(2,1)S(1)}, bf16[2,2,256,256]{3,2,1,0:T(8,128)(2,1)S(1)}, u32[]{:S(2)}, u32[]{:S(2)}) collective-permute-start(bf16[2,2,256,256]{3,2,1,0:T(8,128)(2,1)S(1)} %get-tuple-element.275.refs_7_.refs_4_), channel_id=1, source_target_pairs={{0,2},{2,4},{4,6},{3,1},{5,3},{7,5},{8,10},{10,12},{12,14},{11,9},... | collective-permute-start | bytes 1572872 | tf_op jit(solution)/shard_map/ppermute | solution.py:367
  203.0 25.9 %collective-permute-start.75 = (bf16[4,2,256,256]{3,2,1,0:T(8,128)(2,1)S(1)}, bf16[4,2,256,256]{3,2,1,0:T(8,128)(2,1)S(1)}, u32[]{:S(2)}, u32[]{:S(2)}) collective-permute-start(bf16[4,2,256,256]{3,2,1,0:T(8,128)(2,1)S(1)} %get-tuple-element.307), channel_id=1, source_target_pairs={{0,16},{8,24},{16,0},{24,8},{1,17},{9,25},{17,1},{25,9},{2,18},{10... | collective-permute-start | bytes 3145736 | tf_op jit(solution)/shard_map/ppermute | solution.py:387
  205.5 11.8 %collective-permute-start.64 = (bf16[2,2,256,256]{3,2,1,0:T(8,128)(2,1)S(1)}, bf16[2,2,256,256]{3,2,1,0:T(8,128)(2,1)S(1)}, u32[]{:S(2)}, u32[]{:S(2)}) collective-permute-start(bf16[2,2,256,256]{3,2,1,0:T(8,128)(2,1)S(1)} %get-tuple-element.278.refs_2_.refs_0_), channel_id=1, source_target_pairs={{0,2},{2,4},{4,6},{3,1},{5,3},{7,5},{8,10},{10,12},{12,14},{11,9},... | collective-permute-start | bytes 1572872 | tf_op jit(solution)/shard_map/ppermute | solution.py:367
  209.7 25.3 %collective-permute-start.72 = (bf16[4,2,256,256]{3,2,1,0:T(8,128)(2,1)S(1)}, bf16[4,2,256,256]{3,2,1,0:T(8,128)(2,1)S(1)}, u32[]{:S(2)}, u32[]{:S(2)}) collective-permute-start(bf16[4,2,256,256]{3,2,1,0:T(8,128)(2,1)S(1)} %collective-permute-done.71.near_ref), channel_id=1, source_target_pairs={{0,1},{1,0},{2,3},{3,2},{4,5},{5,4},{6,7},{7,6},{8,9},{9,8},{10,11... | collective-permute-start | bytes 3145736 | tf_op jit(solution)/shard_map/ppermute | solution.py:390
  224.6 11.6 %collective-permute-start.73 = (bf16[2,2,256,256]{3,2,1,0:T(8,128)(2,1)S(1)}, bf16[2,2,256,256]{3,2,1,0:T(8,128)(2,1)S(1)}, u32[]{:S(2)}, u32[]{:S(2)}) collective-permute-start(bf16[2,2,256,256]{3,2,1,0:T(8,128)(2,1)S(1)} %get-tuple-element.294.refs_7_.refs_4_), channel_id=1, source_target_pairs={{0,2},{2,4},{4,6},{3,1},{5,3},{7,5},{8,10},{10,12},{12,14},{11,9},... | collective-permute-start | bytes 1572872 | tf_op jit(solution)/shard_map/ppermute | solution.py:367
  228.9 18.5 %collective-permute-start.76 = (bf16[4,2,256,256]{3,2,1,0:T(8,128)(2,1)S(1)}, bf16[4,2,256,256]{3,2,1,0:T(8,128)(2,1)S(1)}, u32[]{:S(2)}, u32[]{:S(2)}) collective-permute-start(bf16[4,2,256,256]{3,2,1,0:T(8,128)(2,1)S(1)} %collective-permute-done.75.near_ref), channel_id=1, source_target_pairs={{0,1},{1,0},{2,3},{3,2},{4,5},{5,4},{6,7},{7,6},{8,9},{9,8},{10,11... | collective-permute-start | bytes 3145736 | tf_op jit(solution)/shard_map/ppermute | solution.py:390
  230.5 12.7 %collective-permute-start.74 = (bf16[2,2,256,256]{3,2,1,0:T(8,128)(2,1)S(1)}, bf16[2,2,256,256]{3,2,1,0:T(8,128)(2,1)S(1)}, u32[]{:S(2)}, u32[]{:S(2)}) collective-permute-start(bf16[2,2,256,256]{3,2,1,0:T(8,128)(2,1)S(1)} %get-tuple-element.297.refs_2_), channel_id=1, source_target_pairs={{0,2},{2,4},{4,6},{3,1},{5,3},{7,5},{8,10},{10,12},{12,14},{11,9},... | collective-permute-start | bytes 1572872 | tf_op jit(solution)/shard_map/ppermute | solution.py:367
  235.0 25.6 %collective-permute-start.88 = (bf16[4,2,256,256]{3,2,1,0:T(8,128)(2,1)S(1)}, bf16[4,2,256,256]{3,2,1,0:T(8,128)(2,1)S(1)}, u32[]{:S(2)}, u32[]{:S(2)}) collective-permute-start(bf16[4,2,256,256]{3,2,1,0:T(8,128)(2,1)S(1)} %get-tuple-element.325), channel_id=1, source_target_pairs={{0,16},{8,24},{16,0},{24,8},{1,17},{9,25},{17,1},{25,9},{2,18},{10... | collective-permute-start | bytes 3145736 | tf_op jit(solution)/shard_map/ppermute | solution.py:387
  239.5 12.4 %collective-permute-start.81 = (bf16[2,2,256,256]{3,2,1,0:T(8,128)(2,1)S(1)}, bf16[2,2,256,256]{3,2,1,0:T(8,128)(2,1)S(1)}, u32[]{:S(2)}, u32[]{:S(2)}) collective-permute-start(bf16[2,2,256,256]{3,2,1,0:T(8,128)(2,1)S(1)} %get-tuple-element.302.refs_5_), channel_id=1, source_target_pairs={{0,2},{2,4},{4,6},{3,1},{5,3},{7,5},{8,10},{10,12},{12,14},{11,9},... | collective-permute-start | bytes 1572872 | tf_op jit(solution)/shard_map/ppermute | solution.py:367
  (49 other events, 346.3 us)
